TPU v7x, 32 devices: a whole 2x2x4 slice. The times are simulated.
32 devices in a mesh: rep: 8 (over z, x), tp: 4 (over y, core).
Axes of the slice: x: 2, y: 2, z: 4, core: 2. Of those that a mesh axis runs over, the one named last changes fastest.
Arguments:
- hidden_in: bfloat16 [256, 3584], P('rep'), may hold values from -6 to 6
- k_cache: bfloat16 [256, 4, 64, 128], P('rep', 'tp'), may hold values from -300 to 300, as said below
- v_cache: bfloat16 [256, 4, 64, 128], P('rep', 'tp'), may hold values from -6 to 6
- lengths: int32 [256], replicated, may hold values from 1 to 127, 16384 in all
- routes: int32 [256, 1], replicated, may hold values from 0 to 7; in each aligned block of 32 rows (0 to 31, 32 to 63, ...) at most 8 rows name the same one
- w_query: bfloat16 [3584, 1024], P(None, 'tp'), may hold values from -0.09375 to 0.09375
- b_query: bfloat16 [1024], P('tp'), may hold values from -3 to 3
- w_key: bfloat16 [3584, 256], P(None, 'tp'), may hold values from -0.09375 to 0.09375
- b_key: bfloat16 [256], P('tp'), may hold values from -3 to 3
- w_value: bfloat16 [3584, 256], P(None, 'tp'), may hold values from -0.09375 to 0.09375
- b_value: bfloat16 [256], P('tp'), may hold values from -3 to 3
- w_out: bfloat16 [1024, 3584], P('tp'), may hold values from -0.1875 to 0.1875
- gain_in: bfloat16 [3584], replicated, may hold values from 0.25 to 1.75
- gain_out: bfloat16 [3584], replicated, may hold values from 0.25 to 1.75
- w_head: bfloat16 [19008, 3584], P(('rep', 'tp')), may hold values from -0.09375 to 0.09375
Outputs:
- final_norm: float32 [512], P(('rep', 'tp'))
- top_logit: float32 [512], P(('rep', 'tp'))
- k_cache_out: bfloat16 [512, 4, 64, 128], P('rep', 'tp')
- v_cache_out: bfloat16 [512, 4, 64, 128], P('rep', 'tp')
Inputs may be any that keep to these rules, and one draw needn't show every extreme that they name: `routes`: within the 32 requests of one replica at most 8 name the same replica, and in every draw some replica is named exactly 8 times by some replica's requests. `k_cache`: keys are already rotated to their positions.
All inputs are finite; a program needn't handle non-finite values.
Results may differ from a plain program's by a relative error of at most 0.0022.
Values may be sent and summed in bfloat16 or wider, within the bound.
A program may use at most 128 MiB of HBM per device.

v0:
```python
import jax
import jax.numpy as jnp
from jax import lax
from jax.sharding import PartitionSpec as P


def swapped(shard, axis, distance):
    return lax.ppermute(shard, axis, [(i, i ^ 1 << distance) for i in range(lax.axis_size(axis))])


def rotate(vals, positions):
    half = vals.shape[-1] // 2
    freq = 1000000.0 ** (-(jnp.arange(half, dtype=jnp.float32) * 2.0 / vals.shape[-1]))
    angle = positions[..., None] * freq
    first = vals[..., :half]
    second = vals[..., half:]
    return jnp.concatenate(
        [
            first * jnp.cos(angle) - second * jnp.sin(angle),
            second * jnp.cos(angle) + first * jnp.sin(angle),
        ],
        axis=-1,
    )


def destinations(routes, n_rep, slots, cap, serve):
    flat = routes[:, 0].reshape(n_rep, slots)
    onehot = (flat[:, :, None] == jnp.arange(n_rep, dtype=jnp.int32)[None, None, :]).astype(
        jnp.int32
    )
    rank = jnp.sum((jnp.cumsum(onehot, axis=1) - onehot) * onehot, axis=2)
    source = jnp.arange(n_rep, dtype=jnp.int32)[:, None]
    return ((flat * serve + source * cap + rank).reshape(-1), flat * cap + rank)


def find_home(dest_flat, targets):
    equal = dest_flat[None, :] == targets[:, None]
    home = jnp.sum(
        jnp.where(equal, jnp.arange(dest_flat.shape[0], dtype=jnp.int32)[None, :], 0), axis=1
    )
    return (home, jnp.any(equal, axis=1))


def fill_buckets(arrays, own_bucket, serve, slots):
    hits = own_bucket[None, :] == jnp.arange(serve, dtype=jnp.int32)[:, None]
    pick = jnp.sum(jnp.where(hits, jnp.arange(slots, dtype=jnp.int32)[None, :], 0), axis=1)
    filled = jnp.any(hits, axis=1)
    return tuple(
        [
            jnp.where(
                filled.reshape((-1,) + (1,) * (item.ndim - 1)),
                item[pick],
                jnp.zeros((), item.dtype),
            )
            for item in arrays
        ]
    )


def write_newest(stored, newest, lens, live_rows, part):
    half_len = stored.shape[1]
    where_pos = part * half_len + jnp.arange(half_len, dtype=jnp.int32)
    written = (where_pos[None, :] == lens[:, None]) & live_rows[:, None]
    return jnp.where(written[:, :, None], newest[:, None, :], stored)


def layer(
    xs,
    keys,
    values,
    lens,
    w_query,
    b_query,
    w_key,
    b_key,
    w_value,
    b_value,
    w_out,
    gain_in,
    gain_out,
    tp_pos,
    n_tp,
):
    eps = 1e-06
    count = xs.shape[0]
    head_size = keys.shape[-1]
    half_len = keys.shape[1]
    part = tp_pos % 2
    even = part == 0
    xf = xs.astype(jnp.float32)
    normed_in = (
        xf * lax.rsqrt(jnp.mean(xf * xf, axis=1, keepdims=True) + eps) * gain_in.astype(jnp.float32)
    ).astype(jnp.bfloat16)
    positions = lens.astype(jnp.float32)[:, None]
    query = (
        jnp.dot(normed_in, w_query, preferred_element_type=jnp.float32)
        + b_query.astype(jnp.float32)
    ).reshape(count, -1, head_size)
    query = rotate(query, positions).astype(jnp.bfloat16)
    key_part = (
        jnp.dot(normed_in, w_key, preferred_element_type=jnp.float32) + b_key.astype(jnp.float32)
    ).astype(jnp.bfloat16)
    value_part = (
        jnp.dot(normed_in, w_value, preferred_element_type=jnp.float32)
        + b_value.astype(jnp.float32)
    ).astype(jnp.bfloat16)
    other_query, other_key, other_value = swapped((query, key_part, value_part), "tp", 0)
    queries = jnp.where(
        even,
        jnp.concatenate([query, other_query], axis=1),
        jnp.concatenate([other_query, query], axis=1),
    )
    key_raw = jnp.where(
        even,
        jnp.concatenate([key_part, other_key], axis=1),
        jnp.concatenate([other_key, key_part], axis=1),
    )
    value_new = jnp.where(
        even,
        jnp.concatenate([value_part, other_value], axis=1),
        jnp.concatenate([other_value, value_part], axis=1),
    )
    key_new = rotate(key_raw.astype(jnp.float32)[:, None, :], positions)[:, 0].astype(jnp.bfloat16)
    scale = 1.0 / head_size**0.5
    scores = jnp.einsum("sgd,spd->sgp", queries, keys, preferred_element_type=jnp.float32) * scale
    place = part * half_len + jnp.arange(half_len, dtype=jnp.int32)
    live = (place[None, :] < lens[:, None])[:, None, :]
    scores = jnp.where(live, scores, -1e30)
    own_score = (
        jnp.einsum("sgd,sd->sg", queries, key_new, preferred_element_type=jnp.float32) * scale
    )
    own_score = jnp.where(even, own_score, -1e30)
    peak = jnp.maximum(jnp.max(scores, axis=2), own_score)
    weights = jnp.where(live, jnp.exp(scores - peak[..., None]), 0.0)
    own_weight = jnp.where(even, jnp.exp(own_score - peak), 0.0)
    total = jnp.sum(weights, axis=2) + own_weight
    mixed = jnp.einsum(
        "sgp,spd->sgd", weights, values.astype(jnp.float32), precision=lax.Precision.HIGHEST
    )
    mixed = mixed + own_weight[..., None] * value_new.astype(jnp.float32)[:, None, :]
    mixed_keep = jnp.where(even, mixed[:, :2], mixed[:, 2:])
    mixed_give = jnp.where(even, mixed[:, 2:], mixed[:, :2])
    peak_keep = jnp.where(even, peak[:, :2], peak[:, 2:])
    peak_give = jnp.where(even, peak[:, 2:], peak[:, :2])
    total_keep = jnp.where(even, total[:, :2], total[:, 2:])
    total_give = jnp.where(even, total[:, 2:], total[:, :2])
    got_mixed, got_peak, got_total = swapped((mixed_give, peak_give, total_give), "tp", 0)
    upper = jnp.maximum(peak_keep, got_peak)
    mine = jnp.exp(peak_keep - upper)
    theirs = jnp.exp(got_peak - upper)
    merged = (mixed_keep * mine[..., None] + got_mixed * theirs[..., None]) / (
        total_keep * mine + got_total * theirs
    )[..., None]
    attn = merged.reshape(count, -1).astype(jnp.bfloat16)
    rows = count // n_tp
    projected = lax.psum_scatter(
        jnp.dot(attn, w_out, preferred_element_type=jnp.float32),
        "tp",
        scatter_dimension=0,
        tiled=True,
    )
    own_x = lax.dynamic_slice_in_dim(xf, tp_pos * rows, rows, 0)
    state = (own_x + projected).astype(jnp.bfloat16)
    sf = state.astype(jnp.float32)
    ms = jnp.mean(sf * sf, axis=1)
    normed = (sf * lax.rsqrt(ms + eps)[:, None] * gain_out.astype(jnp.float32)).astype(jnp.bfloat16)
    return (normed, jnp.sqrt(ms), rows, key_new, value_new)


def per_device(
    hidden_in,
    k_cache,
    v_cache,
    lengths,
    routes,
    w_query,
    b_query,
    w_key,
    b_key,
    w_value,
    b_value,
    w_out,
    gain_in,
    gain_out,
    w_head,
):
    n_rep = lax.axis_size("rep")
    n_tp = lax.axis_size("tp")
    rep_pos = lax.axis_index("rep")
    tp_pos = lax.axis_index("tp")
    part = tp_pos % 2
    slots = hidden_in.shape[0]
    cap = max(2, 2 * slots // n_rep)
    serve = n_rep * cap
    dest_flat, bucket_grid = destinations(routes, n_rep, slots, cap, serve)
    own_bucket = lax.dynamic_slice_in_dim(bucket_grid, rep_pos, 1, 0)[0]
    keys_home = k_cache[:, 0]
    values_home = v_cache[:, 0]
    weights_all = (w_query, b_query, w_key, b_key, w_value, b_value, w_out, gain_in, gain_out)
    send_x, send_k, send_v = fill_buckets(
        (hidden_in, keys_home, values_home), own_bucket, serve, slots
    )
    got_x, got_k, got_v = (
        lax.all_to_all(send_x, "rep", split_axis=0, concat_axis=0, tiled=True),
        lax.all_to_all(send_k, "rep", split_axis=0, concat_axis=0, tiled=True),
        lax.all_to_all(send_v, "rep", split_axis=0, concat_axis=0, tiled=True),
    )
    targets = rep_pos * serve + jnp.arange(serve, dtype=jnp.int32)
    home, valid = find_home(dest_flat, targets)
    lens = jnp.where(valid, lengths[home], 0)
    normed, norm_own, rows, key_new, value_new = layer(
        got_x, got_k, got_v, lens, *weights_all, tp_pos, n_tp
    )
    keys_served = write_newest(got_k, key_new, lens, valid, part)
    values_served = write_newest(got_v, value_new, lens, valid, part)
    logits = lax.dot_general(
        lax.all_gather(normed, ("rep", "tp"), axis=0, tiled=True),
        w_head,
        (((1,), (1,)), ((), ())),
        preferred_element_type=jnp.float32,
    )
    partial_value = jnp.max(logits, axis=1)
    top_all = lax.pmax(partial_value, ("rep", "tp"))
    own_valid = lax.dynamic_slice_in_dim(valid, tp_pos * rows, rows, 0)
    top_own = lax.dynamic_slice_in_dim(top_all, (rep_pos * n_tp + tp_pos) * rows, rows, 0)
    final_norm = jnp.where(own_valid, norm_own, 0.0)
    top_logit = jnp.where(own_valid, top_own, 0.0)
    return (final_norm, top_logit, keys_served[:, None], values_served[:, None])


def solution(mesh):
    in_specs = (
        P("rep", None),
        P("rep", "tp", None, None),
        P("rep", "tp", None, None),
        P(),
        P(),
        P(None, "tp"),
        P("tp"),
        P(None, "tp"),
        P("tp"),
        P(None, "tp"),
        P("tp"),
        P("tp", None),
        P(),
        P(),
        P(("rep", "tp"), None),
    )
    out_specs = (
        P(("rep", "tp")),
        P(("rep", "tp")),
        P("rep", "tp", None, None),
        P("rep", "tp", None, None),
    )
    return jax.shard_map(
        per_device, mesh=mesh, in_specs=in_specs, out_specs=out_specs, check_vma=False
    )
```

profile of v0, /device:TPU:0, one launch (start us, length us, event | category | flops | bytes accessed | tf_op | source)
XLA Modules:
  0.0 237.7 jit_solution(15469448627704497283)
XLA Ops:
  7.7 1.4 broadcast_multiply_fusion
  10.8 2.3 gather_fusion
  13.1 0.9 bitcast_select_fusion
  14.0 7.3 %all-to-all-start = ((bf16[8,8,3584]{2,1,0:T(8,128)(2,1)}), bf16[8,8,3584]{2,1,0:T(8,128)(2,1)S(1)}, u32[]{:S(2)}, u32[]{:S(2)}) async-start(bf16[8,8,3584]{2,1,0:T(8,128)(2,1)} %bitcast_select_fusion), calls=%async_computation | async-start | bytes 917504 | tf_op jit(solution)/shard_map/all_to_all | solution.py:204
  21.6 1.8 gather_fusion.3
  23.4 2.7 %gather_fusion.2 = bf16[64,64,128]{2,1,0:T(8,128)(2,1)} fusion(bf16[32,64,128]{2,1,0:T(8,128)(2,1)} %bitcast.53, s32[1024]{0:T(1024)S(1)} %pad_clamp_fusion.1), kind=kCustom, calls=%fused_computation.2 | custom fusion | bytes 2097408 | tf_op jit(solution)/shard_map/gather | solution.py:52
  26.1 0.8 gather_fusion.1
  26.9 0.8 multiply_cosine_fusion.1
  27.7 2.7 %broadcast_select_fusion.1 = (bf16[64,64,128]{2,1,0:T(8,128)(2,1)}, bf16[64,64,128]{2,1,0:T(8,128)(2,1)}) fusion(bf16[64,64,128]{2,1,0:T(8,128)(2,1)} %gather_fusion.2, pred[64]{0:T(512)(128)(4,1)S(1)} %fusion.33, bf16[64,64,128]{2,1,0:T(8,128)(2,1)S(1)} %gather_fusion.3), kind=kLoop, calls=%fused_computation.20 | loop fusion | flops 1048576 | bytes 4194368 | tf_op jit(solution)/shard_map/jit(_where)/select_n | solution.py:50
  30.4 3.9 %all-to-all-done = bf16[8,8,3584]{2,1,0:T(8,128)(2,1)S(1)} async-done(((bf16[8,8,3584]{2,1,0:T(8,128)(2,1)}), bf16[8,8,3584]{2,1,0:T(8,128)(2,1)S(1)}, u32[]{:S(2)}, u32[]{:S(2)}) %all-to-all-start) | async-done | bytes 458784 | tf_op jit(solution)/shard_map/all_to_all | solution.py:204
  34.3 3.6 %all-to-all-start.1 = ((bf16[64,64,128]{2,1,0:T(8,128)(2,1)}), bf16[64,64,128]{2,1,0:T(8,128)(2,1)S(1)}, u32[]{:S(2)}, u32[]{:S(2)}) async-start(bf16[64,64,128]{2,1,0:T(8,128)(2,1)} %get-tuple-element.53), calls=%async_computation.1 | async-start | bytes 2097152 | tf_op jit(solution)/shard_map/all_to_all | solution.py:205
  38.3 2.1 fusion.3
  40.4 1.9 fusion.2
  43.4 0.9 subtract_convert_fusion
  44.5 0.9 fusion.32
  45.4 1.5 fusion.40
  46.9 16.9 %all-to-all-done.1 = bf16[64,64,128]{2,1,0:T(8,128)(2,1)S(1)} async-done(((bf16[64,64,128]{2,1,0:T(8,128)(2,1)}), bf16[64,64,128]{2,1,0:T(8,128)(2,1)S(1)}, u32[]{:S(2)}, u32[]{:S(2)}) %all-to-all-start.1) | async-done | bytes 1048608 | tf_op jit(solution)/shard_map/all_to_all | solution.py:205
  63.8 4.2 %all-to-all-start.2 = ((bf16[64,64,128]{2,1,0:T(8,128)(2,1)}), bf16[64,64,128]{2,1,0:T(8,128)(2,1)}, u32[]{:S(2)}, u32[]{:S(2)}) async-start(bf16[64,64,128]{2,1,0:T(8,128)(2,1)} %get-tuple-element.54), calls=%async_computation.2 | async-start | bytes 2097152 | tf_op jit(solution)/shard_map/all_to_all | solution.py:206
  68.1 0.9 fusion.21
  69.1 1.2 fusion.29
  70.3 1.6 fusion.43
  74.1 19.6 %all-to-all-done.2 = bf16[64,64,128]{2,1,0:T(8,128)(2,1)} async-done(((bf16[64,64,128]{2,1,0:T(8,128)(2,1)}), bf16[64,64,128]{2,1,0:T(8,128)(2,1)}, u32[]{:S(2)}, u32[]{:S(2)}) %all-to-all-start.2) | async-done | bytes 1048608 | tf_op jit(solution)/shard_map/all_to_all | solution.py:206
  93.7 2.2 convolution_add_fusion
  96.0 0.9 multiply_add_fusion
  97.6 1.4 fusion.26
  99.0 1.0 convert_bitcast_fusion
  100.0 22.0 %reduce-scatter.2.cloned.1.call-done = f32[16,3584]{1,0:T(8,128)} async-done(((f32[64,3584]{1,0:T(8,128)}), f32[16,3584]{1,0:T(8,128)}) %reduce-scatter.2.cloned.1.call-update) | async-done | bytes 229392 | tf_op jit(solution)/shard_map/reduce_scatter | solution.py:156
  122.0 1.2 fusion.5
  124.0 3.6 %select_bitcast_fusion = (bf16[64,1,64,128]{3,2,1,0:T(8,128)(2,1)}, bf16[64,1,64,128]{3,2,1,0:T(8,128)(2,1)}) fusion(bf16[64,64,128]{2,1,0:T(8,128)(2,1)} %all-to-all-done.2, pred[64,64]{1,0:T(8,128)(4,1)S(1)} %get-tuple-element.45, bf16[64,128]{1,0:T(8,128)(2,1)S(1)} %get-tuple-element.36, bf16[64,64,128]{2,1,0:T(8,128)(2,1)S(1)} %all-to-all-done.1, ...), kind=kLoop, calls=%fused_computation.17 | loop fusion | flops 1048576 | bytes 4231168
  127.6 58.0 %all-gather.2.cloned.1.call-done = bf16[512,3584]{1,0:T(8,128)(2,1)} async-done(((bf16[16,3584]{1,0:T(8,128)(2,1)}), bf16[512,3584]{1,0:T(8,128)(2,1)}) %all-gather.2.cloned.1.call-update) | async-done | bytes 3670032 | tf_op jit(solution)/shard_map/all_gather | solution.py:217
  185.6 5.8 %convolution_reduce_fusion = f32[512]{0:T(512)S(1)} fusion(bf16[512,3584]{1,0:T(8,128)(2,1)} %all-gather.2.cloned.1.call-done, bf16[594,3584]{1,0:T(8,128)(2,1)} %param.29), kind=kOutput, calls=%fused_computation.4 | convolution fusion | flops 2180293120 | bytes 7929856 | tf_op jit(solution)/shard_map/dot_general | solution.py:216
  191.4 38.9 %pmax.7 = f32[512]{0:T(512)S(1)} all-reduce(f32[512]{0:T(512)S(1)} %convolution_reduce_fusion), channel_id=1, replica_groups=mesh['rep'=8,'tp'=4] {'rep','tp'}, use_global_device_ids=true, to_apply=%region_12.13 | all-reduce | flops 512 | bytes 4096 | tf_op jit(solution)/shard_map/pmax | solution.py:223
  (90 shorter events, 8.6 us)
Async XLA Ops:
  7.2 90.4 %copy-start = (bf16[256,3584]{1,0:T(8,128)(2,1)S(1)}, bf16[256,3584]{1,0:T(8,128)(2,1)}, u32[]{:S(2)}) copy-start(bf16[256,3584]{1,0:T(8,128)(2,1)} %param.26) | copy-start | bytes 5505028
  13.0 8.4 %copy-start.10 = (bf16[64]{0:T(256)(128)(2,1)S(1)}, bf16[64]{0:T(256)(128)(2,1)}, u32[]{:S(2)}) copy-start(bf16[64]{0:T(256)(128)(2,1)} %param.23) | copy-start | bytes 388
  13.1 8.4 %copy-start.11 = (bf16[64]{0:T(256)(128)(2,1)S(1)}, bf16[64]{0:T(256)(128)(2,1)}, u32[]{:S(2)}) copy-start(bf16[64]{0:T(256)(128)(2,1)} %param.25) | copy-start | bytes 388
  13.1 8.4 %copy-start.12 = (bf16[256]{0:T(256)(128)(2,1)S(1)}, bf16[256]{0:T(256)(128)(2,1)}, u32[]{:S(2)}) copy-start(bf16[256]{0:T(256)(128)(2,1)} %param.21) | copy-start | bytes 1540
  13.1 8.5 %copy-start.4 = (bf16[3584]{0:T(1024)(128)(2,1)S(1)}, bf16[3584]{0:T(1024)(128)(2,1)}, u32[]{:S(2)}) copy-start(bf16[3584]{0:T(1024)(128)(2,1)} %param.27) | copy-start | bytes 21508
  14.0 20.3 %all-to-all-start = ((bf16[8,8,3584]{2,1,0:T(8,128)(2,1)}), bf16[8,8,3584]{2,1,0:T(8,128)(2,1)S(1)}, u32[]{:S(2)}, u32[]{:S(2)}) async-start(bf16[8,8,3584]{2,1,0:T(8,128)(2,1)} %bitcast_select_fusion), calls=%async_computation | async-start | bytes 917504 | tf_op jit(solution)/shard_map/all_to_all | solution.py:204
  21.2 5.6 %copy-start.9 = (f32[64]{0:T(128)}, f32[64]{0:T(128)S(1)}, u32[]{:S(2)}) copy-start(f32[64]{0:T(128)S(1)} %negate_power_fusion) | copy-start | bytes 772
  21.4 16.5 %copy-start.6 = (pred[64]{0:T(512)(128)(4,1)}, pred[64]{0:T(512)(128)(4,1)S(1)}, u32[]{:S(2)}) copy-start(pred[64]{0:T(512)(128)(4,1)S(1)} %compare_reduce_fusion) | copy-start | bytes 196
  21.6 4.5 %copy-start.1 = (s32[256]{0:T(256)S(1)}, s32[256]{0:T(256)}, u32[]{:S(2)}) copy-start(s32[256]{0:T(256)} %param.18) | copy-start | bytes 3076
  26.9 3.6 %copy-start.8 = (f32[64]{0:T(128)}, f32[64]{0:T(128)S(1)}, u32[]{:S(2)}) copy-start(f32[64]{0:T(128)S(1)} %get-tuple-element.37) | copy-start | bytes 772
  34.3 29.5 %all-to-all-start.1 = ((bf16[64,64,128]{2,1,0:T(8,128)(2,1)}), bf16[64,64,128]{2,1,0:T(8,128)(2,1)S(1)}, u32[]{:S(2)}, u32[]{:S(2)}) async-start(bf16[64,64,128]{2,1,0:T(8,128)(2,1)} %get-tuple-element.53), calls=%async_computation.1 | async-start | bytes 2097152 | tf_op jit(solution)/shard_map/all_to_all | solution.py:205
  38.3 4.5 %copy-start.2 = (bf16[3584,256]{1,0:T(8,128)(2,1)S(1)}, bf16[3584,256]{1,0:T(8,128)(2,1)}, u32[]{:S(2)}) copy-start(bf16[3584,256]{1,0:T(8,128)(2,1)} %param.20) | copy-start | bytes 5505028
  40.4 5.0 %collective-permute-start.2 = (bf16[64,64]{1,0:T(8,128)(2,1)}, bf16[64,64]{1,0:T(8,128)(2,1)}, u32[]{:S(2)}, u32[]{:S(2)}) collective-permute-start(bf16[64,64]{1,0:T(8,128)(2,1)} %fusion.3), channel_id=1, source_target_pairs={{0,1},{1,0},{2,3},{3,2},{4,5},{5,4},{6,7},{7,6},{8,9},{9,8},{10,11... | collective-permute-start | bytes 24584 | tf_op jit(solution)/shard_map/ppermute | solution.py:8
  42.3 2.2 collective-permute-start.1
  44.4 24.6 %collective-permute-start = (bf16[64,2,128]{2,1,0:T(2,128)(2,1)S(1)}, bf16[64,2,128]{2,1,0:T(2,128)(2,1)}, u32[]{:S(2)}, u32[]{:S(2)}) collective-permute-start(bf16[64,2,128]{2,1,0:T(2,128)(2,1)S(1)} %pad_maximum_fusion), channel_id=1, source_target_pairs={{0,1},{1,0},{2,3},{3,2},{4,5},{5,4},{6,7},{7,6},{8,9},{9,8},{10,11... | collective-permute-start | bytes 98312 | tf_op jit(solution)/shard_map/ppermute | solution.py:8
  63.8 29.9 %all-to-all-start.2 = ((bf16[64,64,128]{2,1,0:T(8,128)(2,1)}), bf16[64,64,128]{2,1,0:T(8,128)(2,1)}, u32[]{:S(2)}, u32[]{:S(2)}) async-start(bf16[64,64,128]{2,1,0:T(8,128)(2,1)} %get-tuple-element.54), calls=%async_computation.2 | async-start | bytes 2097152 | tf_op jit(solution)/shard_map/all_to_all | solution.py:206
  68.1 53.9 %reduce-scatter.2.cloned.1.call-start = ((), (), s32[]{:S(2)}) async-start(), calls=%async_computation.4 | async-start | bytes 1146880 | tf_op jit(solution)/shard_map/reduce_scatter | solution.py:156
  71.9 1.0 copy-start.3
  72.6 23.4 %collective-permute-start.3 = (f32[64,2]{1,0:T(8,128)}, f32[64,2]{1,0:T(8,128)}, u32[]{:S(2)}, u32[]{:S(2)}) collective-permute-start(f32[64,2]{1,0:T(8,128)} %slice_select_fusion.1), channel_id=1, source_target_pairs={{0,1},{1,0},{2,3},{3,2},{4,5},{5,4},{6,7},{7,6},{8,9},{9,8},{10,11... | collective-permute-start | bytes 1544 | tf_op jit(solution)/shard_map/ppermute | solution.py:8
  73.6 22.4 %collective-permute-start.5 = (f32[64,2]{1,0:T(8,128)}, f32[64,2]{1,0:T(8,128)}, u32[]{:S(2)}, u32[]{:S(2)}) collective-permute-start(f32[64,2]{1,0:T(8,128)} %slice_select_fusion), channel_id=1, source_target_pairs={{0,1},{1,0},{2,3},{3,2},{4,5},{5,4},{6,7},{7,6},{8,9},{9,8},{10,11... | collective-permute-start | bytes 1544 | tf_op jit(solution)/shard_map/ppermute | solution.py:8
  95.9 1.3 collective-permute-start.4
  97.5 1.5 copy-start.5
  99.0 86.7 %all-gather.2.cloned.1.call-start = ((), (), s32[]{:S(2)}) async-start(), calls=%async_computation.5 | async-start | bytes 3784704 | tf_op jit(solution)/shard_map/all_gather | solution.py:217
  127.6 102.7 %copy-start.7 = (pred[64]{0:T(512)(128)(4,1)S(1)}, pred[64]{0:T(512)(128)(4,1)}, u32[]{:S(2)}) copy-start(pred[64]{0:T(512)(128)(4,1)} %copy-done.6) | copy-start | bytes 196
Sparse Core Ops, SparseCore 0:
  99.1 22.8 reduce-scatter.1
  125.2 60.3 all-gather.1
where the time goes:
time: 239 us; the launch traced here: 238 us
  waiting for transfers between devices  121 us (51%)
  blocking collectives  38.9 us (16%)
  other arithmetic  21.8 us (9%)
  matrix products  16.7 us (7%)
  starting transfers between devices  16.4 us (7%)
  between operations  14.5 us (6%)
  local copies, waits for them, and re-layouts  8.78 us (4%)
    all_gather x1, waiting for transfers between devices, per_device(): lax.all_gather(normed, ('rep', 'tp'), axis=0, tiled=True)  58 us
    pmax x1, blocking collectives, per_device(): top_all = lax.pmax(partial_value, ('rep', 'tp'))  38.9 us
    reduce_scatter x1, waiting for transfers between devices, layer(): lax.psum_scatter(jnp.dot(attn, w_out, preferred_element_type=jnp.float32)...  22 us
    all_to_all x1, waiting for transfers between devices, per_device(): lax.all_to_all(send_v, 'rep', split_axis=0, concat_axis=0, tiled=True)  19.6 us
    all_to_all x1, waiting for transfers between devices, per_device(): lax.all_to_all(send_k, 'rep', split_axis=0, concat_axis=0, tiled=True)  16.9 us
    all_to_all x1, starting transfers between devices, per_device(): lax.all_to_all(send_x, 'rep', split_axis=0, concat_axis=0, tiled=True)  7.25 us
    gather x3, local copies, waits for them, and re-layouts, fill_buckets(): item[pick]  6.74 us
    dot_general x1, matrix products, per_device(): lax.dot_general(lax.all_gather(normed, ('rep', 'tp'), axis=0, tiled=True)...  5.77 us
  transfers between devices with their start and end apart: 11, of which 6 were waited for; matrix products, arithmetic and copies ran while one was open for 13% of the time, Pallas kernels for 0%

commit v1 on v0

--- a/solution.py
+++ b/solution.py
@@ -167,6 +167,15 @@
     return (normed, jnp.sqrt(ms), rows, key_new, value_new)
 
 
+def spread(item, axis):
+    return lax.all_to_all(item, axis, split_axis=0, concat_axis=0, tiled=True)
+
+
+def choose_own(row, wanted, dest_flat, like):
+    hits = dest_flat[None, :] == wanted[:, None]
+    return jnp.sum(jnp.where(hits, row[None, :], 0.0), axis=1).astype(like)
+
+
 def per_device(
     hidden_in,
     k_cache,
@@ -197,34 +206,39 @@
     keys_home = k_cache[:, 0]
     values_home = v_cache[:, 0]
     weights_all = (w_query, b_query, w_key, b_key, w_value, b_value, w_out, gain_in, gain_out)
-    send_x, send_k, send_v = fill_buckets(
-        (hidden_in, keys_home, values_home), own_bucket, serve, slots
-    )
-    got_x, got_k, got_v = (
-        lax.all_to_all(send_x, "rep", split_axis=0, concat_axis=0, tiled=True),
-        lax.all_to_all(send_k, "rep", split_axis=0, concat_axis=0, tiled=True),
-        lax.all_to_all(send_v, "rep", split_axis=0, concat_axis=0, tiled=True),
-    )
+    send_k, send_v = fill_buckets((keys_home, values_home), own_bucket, serve, slots)
+    got_k, got_v = spread(send_k, "rep"), spread(send_v, "rep")
+    home_lens = lax.dynamic_slice_in_dim(lengths, rep_pos * slots, slots, 0)
+    normed, norm_own, rows, key_new, value_new = layer(
+        hidden_in, keys_home, values_home, home_lens, *weights_all, tp_pos, n_tp
+    )
+    (send_new,) = fill_buckets(
+        (jnp.concatenate([key_new, value_new], axis=1),), own_bucket, serve, slots
+    )
+    got_new = spread(send_new, "rep")
+    head_size = key_new.shape[1]
     targets = rep_pos * serve + jnp.arange(serve, dtype=jnp.int32)
     home, valid = find_home(dest_flat, targets)
     lens = jnp.where(valid, lengths[home], 0)
-    normed, norm_own, rows, key_new, value_new = layer(
-        got_x, got_k, got_v, lens, *weights_all, tp_pos, n_tp
-    )
-    keys_served = write_newest(got_k, key_new, lens, valid, part)
-    values_served = write_newest(got_v, value_new, lens, valid, part)
+    keys_served = write_newest(got_k, got_new[:, :head_size], lens, valid, part)
+    values_served = write_newest(got_v, got_new[:, head_size:], lens, valid, part)
     logits = lax.dot_general(
+        w_head,
         lax.all_gather(normed, ("rep", "tp"), axis=0, tiled=True),
-        w_head,
         (((1,), (1,)), ((), ())),
         preferred_element_type=jnp.float32,
     )
-    partial_value = jnp.max(logits, axis=1)
-    top_all = lax.pmax(partial_value, ("rep", "tp"))
-    own_valid = lax.dynamic_slice_in_dim(valid, tp_pos * rows, rows, 0)
-    top_own = lax.dynamic_slice_in_dim(top_all, (rep_pos * n_tp + tp_pos) * rows, rows, 0)
-    final_norm = jnp.where(own_valid, norm_own, 0.0)
-    top_logit = jnp.where(own_valid, top_own, 0.0)
+    norm_all = lax.dynamic_update_slice_in_dim(
+        jnp.zeros((n_rep * slots,), jnp.float32),
+        norm_own,
+        (rep_pos * n_tp + tp_pos) * rows,
+        0,
+    )
+    both = lax.pmax(jnp.stack([jnp.max(logits, axis=0), norm_all]), ("rep", "tp"))
+    share = serve // n_tp
+    wanted = (rep_pos * n_tp + tp_pos) * share + jnp.arange(share, dtype=jnp.int32)
+    final_norm = choose_own(both[1], wanted, dest_flat, jnp.float32)
+    top_logit = choose_own(both[0], wanted, dest_flat, jnp.float32)
     return (final_norm, top_logit, keys_served[:, None], values_served[:, None])
 
 

time: 239 us -> 176 us (0.74)
  waiting for transfers between devices: 121 us -> 68.5 us
  matrix products: 16.7 us -> 11.6 us
  other arithmetic: 21.8 us -> 18.1 us
  local copies, waits for them, and re-layouts: 8.78 us -> 6.22 us
    all_gather x1, waiting for transfers between devices: 58 us -> 3.16 us  [per_device(): lax.all_gather(normed, ('rep', 'tp'), axis=0, tiled=True)]
    all_to_all x3, waiting for transfers between devices: 40.3 us -> 55.1 us  [spread(): return lax.all_to_all(item, axis, split_axis=0, concat_axis=0, tiled=True)]
    reduce_scatter x1, waiting for transfers between devices: 22 us -> 9.11 us  [layer(): lax.psum_scatter(jnp.dot(attn, w_out, preferred_element_type=jnp.float32)...]
    broadcast_in_dim x0 -> x1, other arithmetic: none -> 3.62 us  [per_device(): return (final_norm, top_logit, keys_served[:, None], values_served[:, None])]
    unnamed x1 -> x0, other arithmetic: 3.6 us -> none
    gather x3, local copies, waits for them, and re-layouts: 6.74 us -> 4.14 us  [fill_buckets(): item[pick]]
  transfers between devices with their start and end apart: 11 -> 11, of which waited for: 6 -> 6; matrix products, arithmetic and copies ran while one was open for 13% -> 14% of each run, Pallas kernels for 0% -> 0%
where the time goes in v1:
time: 176 us
  waiting for transfers between devices  68.5 us (39%)
  blocking collectives  38.2 us (22%)
  starting transfers between devices  18.6 us (11%)
  other arithmetic  18.1 us (10%)
  between operations  14.3 us (8%)
  matrix products  11.6 us (7%)
  local copies, waits for them, and re-layouts  6.22 us (4%)
    all_to_all x3, waiting for transfers between devices, spread(): return lax.all_to_all(item, axis, split_axis=0, concat_axis=0, tiled=True)  55.1 us
    pmax x1, blocking collectives, per_device(): lax.pmax(jnp.stack([jnp.max(logits, axis=0), norm_all]), ('rep', 'tp'))  38.2 us
    all_to_all x3, starting transfers between devices, spread(): return lax.all_to_all(item, axis, split_axis=0, concat_axis=0, tiled=True)  16.7 us
    reduce_scatter x1, waiting for transfers between devices, layer(): lax.psum_scatter(jnp.dot(attn, w_out, preferred_element_type=jnp.float32)...  9.11 us
    gather x3, local copies, waits for them, and re-layouts, fill_buckets(): item[pick]  4.14 us
    dot_general x1, matrix products, per_device(): lax.dot_general(w_head, lax.all_gather(normed, ('rep', 'tp'), axis=0, til...  4.09 us
    broadcast_in_dim x1, other arithmetic, per_device(): return (final_norm, top_logit, keys_served[:, None], values_served[:, None])  3.62 us
    select_n x2, other arithmetic, fill_buckets(): jnp.where(filled.reshape((-1,) + (1,) * (item.ndim - 1)), item[pick], jnp...  3.54 us
  transfers between devices with their start and end apart: 11, of which 6 were waited for; matrix products, arithmetic and copies ran while one was open for 14% of the time, Pallas kernels for 0%

profile of v1, /device:TPU:0, one launch (start us, length us, event | category | flops | bytes accessed | tf_op | source)
XLA Modules:
  0.0 175.6 jit_solution(9071596222790802919)
XLA Ops:
  7.2 0.8 convert_element_type.81
  8.1 1.1 multiply_reduce_fusion
  9.2 0.7 convert_element_type.73
  9.9 1.5 fusion.3
  11.9 0.7 convert_element_type.77
  12.5 1.5 fusion.2
  14.1 0.7 convert_element_type.75
  14.8 2.0 %convolution_add_fusion.1 = f32[32,256]{1,0:T(8,128)S(1)} fusion(bf16[3584,256]{1,0:T(8,128)(2,1)} %param.20, f32[256]{0:T(256)S(1)} %convert_element_type.75, f32[3584]{0:T(1024)S(1)} %convert_element_type.73, f32[32]{0:T(128)S(1)} %add_rsqrt_fusion.1, bf16[32,3584]{1,0:T(8,128)(2,1)S(1)} %copy-done.4), kind=kOutput, calls=%fused_computation.10 | convolution fusion | flops 59187200 | bytes 2112640 | tf_op jit(solution)/shard_map/dot_general | solution.py:96
  18.4 0.7 broadcast_multiply_fusion
  19.2 0.7 fusion.50
  20.3 0.8 convert_element_type.72
  24.2 1.0 collective-permute-done.4
  25.4 1.2 fusion.27
  26.6 0.7 gather_fusion.3
  27.4 2.7 %gather_fusion.2 = bf16[64,64,128]{2,1,0:T(8,128)(2,1)} fusion(bf16[32,64,128]{2,1,0:T(8,128)(2,1)} %bitcast.51, s32[1024]{0:T(1024)S(1)} %pad_clamp_fusion), kind=kCustom, calls=%fused_computation.2 | custom fusion | bytes 2097408 | tf_op jit(solution)/shard_map/gather | solution.py:52
  30.1 2.9 %broadcast_select_fusion = (bf16[64,64,128]{2,1,0:T(8,128)(2,1)}, bf16[64,64,128]{2,1,0:T(8,128)(2,1)}) fusion(bf16[64,64,128]{2,1,0:T(8,128)(2,1)S(1)} %gather_fusion.3, pred[64]{0:T(512)(128)(4,1)S(1)} %fusion.30, bf16[64,64,128]{2,1,0:T(8,128)(2,1)} %gather_fusion.2), kind=kLoop, calls=%fused_computation.17 | loop fusion | flops 1048576 | bytes 4194368 | tf_op jit(solution)/shard_map/jit(_where)/select_n | solution.py:50
  32.9 0.7 gather_fusion.1
  33.6 0.7 bitcast_select_fusion
  34.3 7.0 %all-to-all-start = ((bf16[8,8,256]{2,1,0:T(8,128)(2,1)}), bf16[8,8,256]{2,1,0:T(8,128)(2,1)S(1)}, u32[]{:S(2)}, u32[]{:S(2)}) async-start(bf16[8,8,256]{2,1,0:T(8,128)(2,1)} %bitcast_select_fusion), calls=%async_computation.1 | async-start | bytes 65536 | tf_op jit(solution)/shard_map/all_to_all | solution.py:171
  41.3 9.1 %reduce-scatter.2.cloned.1.call-done = f32[8,3584]{1,0:T(8,128)} async-done(((f32[32,3584]{1,0:T(8,128)}), f32[8,3584]{1,0:T(8,128)}) %reduce-scatter.2.cloned.1.call-update) | async-done | bytes 114704 | tf_op jit(solution)/shard_map/reduce_scatter | solution.py:156
  50.4 1.1 fusion.5
  51.5 5.5 %all-to-all-start.2 = ((bf16[64,64,128]{2,1,0:T(8,128)(2,1)}), bf16[64,64,128]{2,1,0:T(8,128)(2,1)S(1)}, u32[]{:S(2)}, u32[]{:S(2)}) async-start(bf16[64,64,128]{2,1,0:T(8,128)(2,1)} %get-tuple-element.33), calls=%async_computation.3 | async-start | bytes 2097152 | tf_op jit(solution)/shard_map/all_to_all | solution.py:171
  57.1 0.7 fusion.7
  57.8 26.1 %all-to-all-done.2 = bf16[64,64,128]{2,1,0:T(8,128)(2,1)S(1)} async-done(((bf16[64,64,128]{2,1,0:T(8,128)(2,1)}), bf16[64,64,128]{2,1,0:T(8,128)(2,1)S(1)}, u32[]{:S(2)}, u32[]{:S(2)}) %all-to-all-start.2) | async-done | bytes 1048608 | tf_op jit(solution)/shard_map/all_to_all | solution.py:171
  83.9 4.2 %all-to-all-start.1 = ((bf16[64,64,128]{2,1,0:T(8,128)(2,1)}), bf16[64,64,128]{2,1,0:T(8,128)(2,1)}, u32[]{:S(2)}, u32[]{:S(2)}) async-start(bf16[64,64,128]{2,1,0:T(8,128)(2,1)} %get-tuple-element.34), calls=%async_computation.2 | async-start | bytes 2097152 | tf_op jit(solution)/shard_map/all_to_all | solution.py:171
  88.6 0.8 gather_fusion
  89.9 29.0 %all-to-all-done.1 = bf16[64,64,128]{2,1,0:T(8,128)(2,1)} async-done(((bf16[64,64,128]{2,1,0:T(8,128)(2,1)}), bf16[64,64,128]{2,1,0:T(8,128)(2,1)}, u32[]{:S(2)}, u32[]{:S(2)}) %all-to-all-start.1) | async-done | bytes 1048608 | tf_op jit(solution)/shard_map/all_to_all | solution.py:171
  118.9 3.6 %select_bitcast_fusion = (bf16[64,1,64,128]{3,2,1,0:T(8,128)(2,1)}, bf16[64,1,64,128]{3,2,1,0:T(8,128)(2,1)}) fusion(bf16[64,64,128]{2,1,0:T(8,128)(2,1)S(1)} %all-to-all-done.2, pred[64,64]{1,0:T(8,128)(4,1)S(1)} %compare_and_fusion, bf16[64,128]{1,0:T(8,128)(2,1)S(1)} %get-tuple-element.19, bf16[64,64,128]{2,1,0:T(8,128)(2,1)} %all-to-all-done.1, ...), kind=kLoop, calls=%fused_computation.15 | loop fusion | flops 1048576 | bytes 4231168 | tf_op jit(solution)/shard_map/broadcast_in_dim | solution.py:242
  122.5 3.2 %all-gather.2.cloned.1.call-done = bf16[256,3584]{1,0:T(8,128)(2,1)} async-done(((bf16[8,3584]{1,0:T(8,128)(2,1)}), bf16[256,3584]{1,0:T(8,128)(2,1)}) %all-gather.2.cloned.1.call-update) | async-done | bytes 1835024 | tf_op jit(solution)/shard_map/all_gather | solution.py:227
  125.7 4.1 %convolution_reduce_fusion = f32[256]{0:T(256)S(1)} fusion(bf16[256,3584]{1,0:T(8,128)(2,1)} %all-gather.2.cloned.1.call-done, bf16[594,3584]{1,0:T(8,128)(2,1)} %param.29), kind=kOutput, calls=%fused_computation.4 | convolution fusion | flops 1090146560 | bytes 6093824 | tf_op jit(solution)/shard_map/dot_general | solution.py:225
  129.8 38.2 %pmax.7 = f32[2,256]{1,0:T(2,128)S(1)} all-reduce(f32[2,256]{1,0:T(2,128)S(1)} %pad_maximum_fusion.3), channel_id=1, replica_groups=mesh['rep'=8,'tp'=4] {'rep','tp'}, use_global_device_ids=true, to_apply=%region_8.9 | all-reduce | flops 512 | bytes 4096 | tf_op jit(solution)/shard_map/pmax | solution.py:237
  168.0 0.7 fusion.20
  (86 shorter events, 6.9 us)
Async XLA Ops:
  7.2 18.2 %copy-start = (bf16[256,3584]{1,0:T(8,128)(2,1)S(1)}, bf16[256,3584]{1,0:T(8,128)(2,1)}, u32[]{:S(2)}) copy-start(bf16[256,3584]{1,0:T(8,128)(2,1)} %param.26) | copy-start | bytes 5505028
  7.2 7.6 %copy-start.4 = (bf16[32,3584]{1,0:T(8,128)(2,1)S(1)}, bf16[32,3584]{1,0:T(8,128)(2,1)}, u32[]{:S(2)}) copy-start(bf16[32,3584]{1,0:T(8,128)(2,1)} %param.15) | copy-start | bytes 688132
  7.2 43.2 %reduce-scatter.2.cloned.1.call-start = ((), (), s32[]{:S(2)}) async-start(), calls=%async_computation.4 | async-start | bytes 573440 | tf_op jit(solution)/shard_map/reduce_scatter | solution.py:156
  9.2 7.7 %copy-start.1 = (s32[256]{0:T(256)S(1)}, s32[256]{0:T(256)}, u32[]{:S(2)}) copy-start(s32[256]{0:T(256)} %param.18) | copy-start | bytes 3076
  9.9 8.5 %copy-start.6 = (s32[256,1]{0,1:T(1,128)S(1)}, s32[256,1]{0,1:T(1,128)}, u32[]{:S(2)}) copy-start(s32[256,1]{0,1:T(1,128)} %param.19) | copy-start | bytes 3076
  11.4 10.0 %collective-permute-start.2 = (bf16[32,64]{1,0:T(8,128)(2,1)S(1)}, bf16[32,64]{1,0:T(8,128)(2,1)S(1)}, u32[]{:S(2)}, u32[]{:S(2)}) collective-permute-start(bf16[32,64]{1,0:T(8,128)(2,1)S(1)} %fusion.3), channel_id=1, source_target_pairs={{0,1},{1,0},{2,3},{3,2},{4,5},{5,4},{6,7},{7,6},{8,9},{9,8},{10,11... | collective-permute-start | bytes 12296 | tf_op jit(solution)/shard_map/ppermute | solution.py:8
  12.5 8.6 %copy-start.5 = (bf16[3584]{0:T(1024)(128)(2,1)S(1)}, bf16[3584]{0:T(1024)(128)(2,1)}, u32[]{:S(2)}) copy-start(bf16[3584]{0:T(1024)(128)(2,1)} %param.28) | copy-start | bytes 21508
  14.0 7.2 %collective-permute-start.1 = (bf16[32,64]{1,0:T(8,128)(2,1)S(1)}, bf16[32,64]{1,0:T(8,128)(2,1)S(1)}, u32[]{:S(2)}, u32[]{:S(2)}) collective-permute-start(bf16[32,64]{1,0:T(8,128)(2,1)S(1)} %fusion.2), channel_id=1, source_target_pairs={{0,1},{1,0},{2,3},{3,2},{4,5},{5,4},{6,7},{7,6},{8,9},{9,8},{10,11... | collective-permute-start | bytes 12296 | tf_op jit(solution)/shard_map/ppermute | solution.py:8
  14.8 7.0 %copy-start.3 = (bf16[32,1,64,128]{3,2,1,0:T(8,128)(2,1)S(1)}, bf16[32,1,64,128]{3,2,1,0:T(8,128)(2,1)}, u32[]{:S(2)}) copy-start(bf16[32,1,64,128]{3,2,1,0:T(8,128)(2,1)} %param.16) | copy-start | bytes 1572868
  16.8 6.4 %copy-start.2 = (bf16[32,1,64,128]{3,2,1,0:T(8,128)(2,1)S(1)}, bf16[32,1,64,128]{3,2,1,0:T(8,128)(2,1)}, u32[]{:S(2)}) copy-start(bf16[32,1,64,128]{3,2,1,0:T(8,128)(2,1)} %param.17) | copy-start | bytes 1572868
  17.3 4.2 %collective-permute-start = (bf16[32,2,128]{2,1,0:T(2,128)(2,1)S(1)}, bf16[32,2,128]{2,1,0:T(2,128)(2,1)S(1)}, u32[]{:S(2)}, u32[]{:S(2)}) collective-permute-start(bf16[32,2,128]{2,1,0:T(2,128)(2,1)S(1)} %pad_maximum_fusion), channel_id=1, source_target_pairs={{0,1},{1,0},{2,3},{3,2},{4,5},{5,4},{6,7},{7,6},{8,9},{9,8},{10,11... | collective-permute-start | bytes 49160 | tf_op jit(solution)/shard_map/ppermute | solution.py:8
  22.8 1.3 collective-permute-start.3
  22.8 1.3 collective-permute-start.5
  23.9 1.3 collective-permute-start.4
  34.3 17.2 %all-to-all-start = ((bf16[8,8,256]{2,1,0:T(8,128)(2,1)}), bf16[8,8,256]{2,1,0:T(8,128)(2,1)S(1)}, u32[]{:S(2)}, u32[]{:S(2)}) async-start(bf16[8,8,256]{2,1,0:T(8,128)(2,1)} %bitcast_select_fusion), calls=%async_computation.1 | async-start | bytes 65536 | tf_op jit(solution)/shard_map/all_to_all | solution.py:171
  51.5 32.4 %all-to-all-start.2 = ((bf16[64,64,128]{2,1,0:T(8,128)(2,1)}), bf16[64,64,128]{2,1,0:T(8,128)(2,1)S(1)}, u32[]{:S(2)}, u32[]{:S(2)}) async-start(bf16[64,64,128]{2,1,0:T(8,128)(2,1)} %get-tuple-element.33), calls=%async_computation.3 | async-start | bytes 2097152 | tf_op jit(solution)/shard_map/all_to_all | solution.py:171
  57.0 68.6 %all-gather.2.cloned.1.call-start = ((), (), s32[]{:S(2)}) async-start(), calls=%async_computation.5 | async-start | bytes 1892352 | tf_op jit(solution)/shard_map/all_gather | solution.py:227
  83.9 35.0 %all-to-all-start.1 = ((bf16[64,64,128]{2,1,0:T(8,128)(2,1)}), bf16[64,64,128]{2,1,0:T(8,128)(2,1)}, u32[]{:S(2)}, u32[]{:S(2)}) async-start(bf16[64,64,128]{2,1,0:T(8,128)(2,1)} %get-tuple-element.34), calls=%async_computation.2 | async-start | bytes 2097152 | tf_op jit(solution)/shard_map/all_to_all | solution.py:171
Sparse Core Ops, SparseCore 0:
  26.7 23.6 reduce-scatter.1
  60.7 64.8 all-gather.1

commit v2 on v1

--- a/solution.py
+++ b/solution.py
@@ -1,6 +1,10 @@
+import functools
+
 import jax
 import jax.numpy as jnp
 from jax import lax
+from jax.experimental import pallas as pl
+from jax.experimental.pallas import tpu as pltpu
 from jax.sharding import PartitionSpec as P
 
 
@@ -242,6 +246,515 @@
     return (final_norm, top_logit, keys_served[:, None], values_served[:, None])
 
 
+MESH = pl.DeviceIdType.MESH
+
+
+def fused(
+    n_rep,
+    n_tp,
+    pick,
+    hid,
+    cosf,
+    sinf,
+    lens,
+    onehot,
+    bq,
+    bk,
+    bv,
+    gin,
+    gout,
+    k_hbm,
+    v_hbm,
+    wq_hbm,
+    wk_hbm,
+    wv_hbm,
+    wo_hbm,
+    wh_hbm,
+    out_k,
+    out_v,
+    out_new,
+    out_max,
+    kz,
+    vz,
+    kb,
+    vb,
+    wq,
+    wk,
+    wv,
+    wo,
+    wh,
+    xf_s,
+    pair,
+    mixed_s,
+    mixed_r,
+    nb,
+    rs_s,
+    rs_b,
+    rs_r,
+    ag,
+    xs,
+    top_s,
+    top_r,
+    top2_s,
+    top2_r,
+    load_sem,
+    keep_sem,
+    cs,
+    cr,
+    ns,
+    nr,
+    ps,
+    pr,
+    rss,
+    rsr,
+    ags,
+    agr,
+    ts,
+    tr,
+):
+    f32, bf16 = jnp.float32, jnp.bfloat16
+    eps = 1e-06
+    rep = lax.axis_index("rep")
+    tp = lax.axis_index("tp")
+    z, x = rep // 2, rep % 2
+    y, c = tp // 2, tp % 2
+    slots, d = hid.shape
+    half_len, hd = kz.shape[1:]
+    cap = kb.shape[0] // n_rep
+    rows = slots // n_tp
+    half_d = d // 2
+    mate = tp + 1 - 2 * c
+    me = rep * n_tp + tp
+
+    def remote(src, dst, send, recv, rep_to, tp_to):
+        return pltpu.make_async_remote_copy(
+            src_ref=src,
+            dst_ref=dst,
+            send_sem=send,
+            recv_sem=recv,
+            device_id=(rep_to, tp_to),
+            device_id_type=MESH,
+        )
+
+    loads = [
+        pltpu.make_async_copy(src, dst, load_sem.at[i])
+        for i, (src, dst) in enumerate(
+            [
+                (k_hbm, kz.at[pl.ds(0, slots)]),
+                (v_hbm, vz.at[pl.ds(0, slots)]),
+                (wq_hbm, wq),
+                (wk_hbm, wk),
+                (wv_hbm, wv),
+                (wo_hbm, wo),
+                (wh_hbm, wh),
+            ]
+        )
+    ]
+    for item in loads:
+        item.start()
+    kz[slots] = jnp.zeros((half_len, hd), bf16)
+    vz[slots] = jnp.zeros((half_len, hd), bf16)
+
+    barrier = pltpu.get_barrier_semaphore()
+    for s in range(1, n_rep):
+        pl.semaphore_signal(
+            barrier, inc=1, device_id=((rep + s) % n_rep, tp), device_id_type=MESH
+        )
+    for s in range(1, n_tp):
+        pl.semaphore_signal(
+            barrier, inc=1, device_id=(rep, (tp + s) % n_tp), device_id_type=MESH
+        )
+    pl.semaphore_wait(barrier, n_rep - 1 + n_tp - 1)
+
+    loads[0].wait()
+    loads[1].wait()
+    sends = []
+    own = pl.ds(rep * cap, cap)
+    for s in list(range(1, n_rep)) + [0]:
+        to = (rep + s) % n_rep
+        there = pl.ds(to * cap, cap)
+        for which, (src, buf, out) in enumerate(((kz, kb, out_k), (vz, vb, out_v))):
+
+            def fill(j, carry, src=src, buf=buf, to=to):
+                buf[to * cap + j] = src[pick[to * cap + j]]
+                return carry
+
+            lax.fori_loop(0, cap, fill, 0)
+            if s:
+                copy = remote(
+                    buf.at[there], out.at[own], cs.at[which, s], cr.at[which, s], to, tp
+                )
+            else:
+                copy = pltpu.make_async_copy(buf.at[own], out.at[own], keep_sem.at[which])
+            copy.start()
+            sends.append((s, which, copy))
+
+    xf = hid[...].astype(f32)
+    xf_s[...] = xf
+    scale_in = lax.rsqrt(jnp.mean(xf * xf, axis=1, keepdims=True) + eps)
+    normed_in = (xf * scale_in * gin[...].astype(f32)).astype(bf16)
+    cos, sin = cosf[...], sinf[...]
+
+    def turn(vals):
+        return vals * cos + pltpu.roll(vals, hd // 2, 1) * sin
+
+    loads[2].wait()
+    query = jnp.dot(normed_in, wq[...], preferred_element_type=f32) + bq[...].astype(f32)
+    loads[3].wait()
+    key_part = jnp.dot(normed_in, wk[...], preferred_element_type=f32) + bk[...].astype(f32)
+    loads[4].wait()
+    value_part = jnp.dot(normed_in, wv[...], preferred_element_type=f32) + bv[...].astype(f32)
+    pair[c] = jnp.concatenate(
+        [
+            turn(query[:, :hd]),
+            turn(query[:, hd:]),
+            jnp.concatenate([key_part, value_part], axis=1),
+        ],
+        axis=0,
+    ).astype(bf16)
+    swap = remote(pair.at[c], pair.at[c], ps.at[0], pr.at[0], rep, mate)
+    swap.start()
+
+    swap.wait_send()
+    remote(pair.at[1 - c], pair.at[1 - c], ps.at[0], pr.at[0], rep, mate).wait_recv()
+    first = pair[0].astype(f32)
+    second = pair[1].astype(f32)
+    queries = jnp.concatenate([first[: 2 * slots], second[: 2 * slots]], axis=0)
+    key_raw = jnp.concatenate(
+        [first[2 * slots :, : hd // 2], second[2 * slots :, : hd // 2]], axis=1
+    )
+    value_new = jnp.concatenate(
+        [first[2 * slots :, hd // 2 :], second[2 * slots :, hd // 2 :]], axis=1
+    )
+    key_new = turn(key_raw).astype(bf16).astype(f32)
+    new_k = jnp.dot(onehot[...], key_new.astype(bf16), preferred_element_type=f32)
+    new_v = jnp.dot(onehot[...], value_new.astype(bf16), preferred_element_type=f32)
+    for t in range(n_rep):
+        cut = slice(t * cap, (t + 1) * cap)
+        nb[t] = jnp.concatenate([new_k[cut], new_v[cut]], axis=0).astype(bf16)
+    new_sends = []
+    for s in range(1, n_rep):
+        to = (rep + s) % n_rep
+        copy = remote(nb.at[to], out_new.at[rep], ns.at[s], nr.at[s], to, tp)
+        copy.start()
+        new_sends.append(copy)
+    out_new[rep] = nb[rep]
+
+    count = 4 * slots
+    scale = 1.0 / hd**0.5
+    keys = kz[0:slots].reshape(slots * half_len, hd)
+    values = vz[0:slots].reshape(slots * half_len, hd)
+    scores = (
+        lax.dot_general(
+            queries.astype(bf16), keys, (((1,), (1,)), ((), ())), preferred_element_type=f32
+        )
+        * scale
+    )
+    row = lax.broadcasted_iota(jnp.int32, scores.shape, 0)
+    col = lax.broadcasted_iota(jnp.int32, scores.shape, 1)
+    live = (col // half_len == row % slots) & (col % half_len + c * half_len < lens[...])
+    scores = jnp.where(live, scores, -1e30)
+    own_score = (
+        jnp.sum(queries * jnp.concatenate([key_new] * 4, axis=0), axis=1, keepdims=True) * scale
+    )
+    even = jnp.broadcast_to(c, (count, 1)) == 0
+    own_score = jnp.where(even, own_score, -1e30)
+    peak = jnp.maximum(jnp.max(scores, axis=1, keepdims=True), own_score)
+    weights = jnp.where(live, jnp.exp(scores - peak), 0.0)
+    own_weight = jnp.where(even, jnp.exp(own_score - peak), 0.0)
+    total = jnp.sum(weights, axis=1, keepdims=True) + own_weight
+    high = weights.astype(bf16)
+    low = (weights - high.astype(f32)).astype(bf16)
+    mixed = jnp.dot(high, values, preferred_element_type=f32) + jnp.dot(
+        low, values, preferred_element_type=f32
+    )
+    mixed = mixed + own_weight * jnp.concatenate([value_new] * 4, axis=0)
+    lane = lax.broadcasted_iota(jnp.int32, (count, hd), 1)
+    stats = jnp.where(lane < hd // 2, peak, total)
+    both = jnp.concatenate([mixed, stats], axis=1)
+    mixed_s[0] = both[: 2 * slots]
+    mixed_s[1] = both[2 * slots :]
+    swap = remote(mixed_s.at[1 - c], mixed_r, ps.at[1], pr.at[1], rep, mate)
+    swap.start()
+    swap.wait()
+    keep = mixed_s[c]
+    got = mixed_r[...]
+    peak_keep, total_keep = keep[:, hd : hd + 1], keep[:, 2 * hd - 1 : 2 * hd]
+    peak_got, total_got = got[:, hd : hd + 1], got[:, 2 * hd - 1 : 2 * hd]
+    upper = jnp.maximum(peak_keep, peak_got)
+    mine = jnp.exp(peak_keep - upper)
+    theirs = jnp.exp(peak_got - upper)
+    merged = (keep[:, :hd] * mine + got[:, :hd] * theirs) / (
+        total_keep * mine + total_got * theirs
+    )
+    attn = jnp.concatenate([merged[:slots], merged[slots:]], axis=1).astype(bf16)
+
+    loads[5].wait()
+    projected = jnp.dot(attn, wo[...], preferred_element_type=f32)
+    for t in range(n_tp):
+        cut = projected[t * rows : (t + 1) * rows]
+        rs_s[t] = jnp.concatenate([cut[:, :half_d], cut[:, half_d:]], axis=0)
+    for t in range(n_tp):
+        rs_b[t] = rs_s[t].astype(bf16)
+    rs_sends = []
+    for s in range(1, n_tp):
+        to = (tp + s) % n_tp
+        copy = remote(rs_b.at[to], rs_r.at[s], rss.at[s], rsr.at[s], rep, to)
+        copy.start()
+        rs_sends.append(copy)
+    summed = rs_s[tp]
+    for s, copy in enumerate(rs_sends):
+        copy.wait()
+        summed = summed + rs_r[s + 1].astype(f32)
+    own_x = xf_s[pl.ds(tp * rows, rows)]
+    state = (
+        (own_x + jnp.concatenate([summed[:rows], summed[rows:]], axis=1)).astype(bf16).astype(f32)
+    )
+    ms = jnp.mean(state * state, axis=1, keepdims=True)
+    normed = state * lax.rsqrt(ms + eps) * gout[...].astype(f32)
+    ag[me] = jnp.concatenate([normed[:, :half_d], normed[:, half_d:]], axis=0).astype(bf16)
+
+    x1, y1 = 1 - x, 1 - y
+    rep_x = rep + 1 - 2 * x
+    tp_y = tp + 2 - 4 * y
+    rep_first, tp_first = c * rep + (1 - c) * rep_x, (1 - c) * tp + c * tp_y
+    rep_second, tp_second = (1 - c) * rep + c * rep_x, c * tp + (1 - c) * tp_y
+    x_first, x_second = c * x + (1 - c) * x1, (1 - c) * x + c * x1
+    n_z = n_rep // 2
+    base_b, base_c, base_d = n_z, 2 * n_z, 4 * n_z
+    ag_sends = []
+
+    def push(block, at, rep_to, tp_to):
+        copy = remote(ag.at[block], ag.at[block], ags.at[at], agr.at[at], rep_to, tp_to)
+        copy.start()
+        ag_sends.append(copy)
+
+    def arrived(block, at):
+        remote(ag.at[block], ag.at[block], ags.at[at], agr.at[at], rep, mate).wait_recv()
+
+    for s in range(1, n_z):
+        push(me, s, ((z + s) % n_z) * 2 + x, tp)
+    plane = [(z + n_z - s) % n_z for s in range(n_z)]
+    for s in range(n_z):
+        block = (plane[s] * 2 + x) * n_tp + tp
+        if s:
+            arrived(block, s)
+        push(block, base_b + s, rep_first, tp_first)
+        push(block, base_c + s, rep_second, tp_second)
+        push(block, base_d + s, rep, mate)
+    for s in range(n_z):
+        block = (plane[s] * 2 + x_first) * n_tp + tp_first
+        arrived(block, base_b + s)
+        push(block, base_c + n_z + s, rep_second, tp_second)
+        push(block, base_d + n_z + s, rep, mate)
+    for s in range(n_z):
+        block = (plane[s] * 2 + x_second) * n_tp + tp_second
+        arrived(block, base_c + s)
+        push(block, base_d + 2 * n_z + s, rep, mate)
+    for s in range(n_z):
+        block = (plane[s] * 2 + x1) * n_tp + tp_y
+        arrived(block, base_c + n_z + s)
+        push(block, base_d + 3 * n_z + s, rep, mate)
+    other_y = mate + 2 - 4 * y
+    x_first_m, x_second_m = x_second, x_first
+    tp_first_m = c * mate + (1 - c) * other_y
+    tp_second_m = (1 - c) * mate + c * other_y
+    for s in range(n_z):
+        arrived((plane[s] * 2 + x) * n_tp + mate, base_d + s)
+        arrived((plane[s] * 2 + x_first_m) * n_tp + tp_first_m, base_d + n_z + s)
+        arrived((plane[s] * 2 + x_second_m) * n_tp + tp_second_m, base_d + 2 * n_z + s)
+        arrived((plane[s] * 2 + x1) * n_tp + other_y, base_d + 3 * n_z + s)
+    for copy in ag_sends:
+        copy.wait_send()
+
+    reqs = n_rep * slots
+    width = 256
+    for i in range(half_d // width):
+        part = ag[:, :, i * width : (i + 1) * width].astype(f32)
+        for h in range(2):
+            xs[:, h * half_d + i * width : h * half_d + (i + 1) * width] = (
+                part[:, h * rows : (h + 1) * rows].reshape(reqs, width).astype(bf16)
+            )
+    loads[6].wait()
+    vocab = wh.shape[0]
+    cuts = list(range(0, vocab, 208)) + [vocab]
+    best = None
+    for low_at, high_at in zip(cuts[:-1], cuts[1:]):
+        logits = lax.dot_general(
+            wh[low_at:high_at], xs[...], (((1,), (1,)), ((), ())), preferred_element_type=f32
+        )
+        one = jnp.max(logits, axis=0, keepdims=True)
+        best = one if best is None else jnp.maximum(best, one)
+    at_row = lax.broadcasted_iota(jnp.int32, (rows, reqs), 0)
+    at_lane = lax.broadcasted_iota(jnp.int32, (rows, reqs), 1)
+    rms = jnp.max(
+        jnp.where(at_lane == at_row + me * rows, jnp.sqrt(ms), 0.0), axis=0, keepdims=True
+    )
+    top = jnp.where(at_row == 0, best, rms)
+    top_s[...] = top
+    hops = []
+    for s in range(1, n_rep):
+        copy = remote(top_s, top_r.at[s], ts.at[s], tr.at[s], (rep + s) % n_rep, tp)
+        copy.start()
+        hops.append(copy)
+    for s, copy in enumerate(hops):
+        copy.wait()
+        top = jnp.maximum(top, top_r[s + 1])
+    top2_s[...] = top
+    hops = []
+    for s in range(1, n_tp):
+        at = n_rep + s
+        copy = remote(top2_s, top2_r.at[s], ts.at[at], tr.at[at], rep, (tp + s) % n_tp)
+        copy.start()
+        hops.append(copy)
+    for s, copy in enumerate(hops):
+        copy.wait()
+        top = jnp.maximum(top, top2_r[s + 1])
+    out_max[...] = top
+
+    for copy in new_sends:
+        copy.wait()
+    for _, _, copy in sends:
+        copy.wait()
+
+
+def fast_device(
+    hidden_in,
+    k_cache,
+    v_cache,
+    lengths,
+    routes,
+    w_query,
+    b_query,
+    w_key,
+    b_key,
+    w_value,
+    b_value,
+    w_out,
+    gain_in,
+    gain_out,
+    w_head,
+):
+    n_rep = lax.axis_size("rep")
+    n_tp = lax.axis_size("tp")
+    rep_pos = lax.axis_index("rep")
+    tp_pos = lax.axis_index("tp")
+    part = tp_pos % 2
+    slots, width = hidden_in.shape
+    half_len, hd = k_cache.shape[2:]
+    cap = max(2, 2 * slots // n_rep)
+    serve = n_rep * cap
+    rows = slots // n_tp
+    reqs = n_rep * slots
+    flat = routes[:, 0].reshape(n_rep, slots)
+    order = jnp.arange(slots, dtype=jnp.int32)
+    before = (flat[:, :, None] == flat[:, None, :]) & (order[None, None, :] < order[None, :, None])
+    rank = jnp.sum(before.astype(jnp.int32), axis=2)
+    source = jnp.arange(n_rep, dtype=jnp.int32)[:, None]
+    dest_flat = (flat * serve + source * cap + rank).reshape(-1)
+    own_bucket = lax.dynamic_slice_in_dim(flat * cap + rank, rep_pos, 1, 0)[0]
+    hits = own_bucket[None, :] == jnp.arange(serve, dtype=jnp.int32)[:, None]
+    pick = slots + jnp.sum(jnp.where(hits, order[None, :] - slots, 0), axis=1)
+    onehot = hits.astype(jnp.bfloat16)
+    home_lens = lax.dynamic_slice_in_dim(lengths, rep_pos * slots, slots, 0)
+    freq = 1000000.0 ** (-(jnp.arange(hd // 2, dtype=jnp.float32) * 2.0 / hd))
+    angle = home_lens.astype(jnp.float32)[:, None] * freq
+    cos, sin = jnp.cos(angle), jnp.sin(angle)
+    cosf = jnp.concatenate([cos, cos], axis=1)
+    sinf = jnp.concatenate([-sin, sin], axis=1)
+    bf16, f32 = jnp.bfloat16, jnp.float32
+    vmem = pl.BlockSpec(memory_space=pltpu.VMEM)
+    anywhere = pl.BlockSpec(memory_space=pl.ANY)
+    dma = pltpu.SemaphoreType.DMA
+    block = (2 * rows, width // 2)
+    got_k, got_v, got_new, best = pl.pallas_call(
+        functools.partial(fused, n_rep, n_tp),
+        out_shape=[
+            jax.ShapeDtypeStruct((serve, half_len, hd), bf16),
+            jax.ShapeDtypeStruct((serve, half_len, hd), bf16),
+            jax.ShapeDtypeStruct((n_rep, 2 * cap, hd), bf16),
+            jax.ShapeDtypeStruct((8, reqs), f32),
+        ],
+        in_specs=[pl.BlockSpec(memory_space=pltpu.SMEM)] + [vmem] * 10 + [anywhere] * 7,
+        out_specs=[anywhere, anywhere, vmem, vmem],
+        scratch_shapes=[
+            pltpu.VMEM((slots + 1, half_len, hd), bf16),
+            pltpu.VMEM((slots + 1, half_len, hd), bf16),
+            pltpu.VMEM((serve, half_len, hd), bf16),
+            pltpu.VMEM((serve, half_len, hd), bf16),
+            pltpu.VMEM(w_query.shape, bf16),
+            pltpu.VMEM(w_key.shape, bf16),
+            pltpu.VMEM(w_value.shape, bf16),
+            pltpu.VMEM(w_out.shape, bf16),
+            pltpu.VMEM(w_head.shape, bf16),
+            pltpu.VMEM((slots, width), f32),
+            pltpu.VMEM((2, 3 * slots, hd), bf16),
+            pltpu.VMEM((2, 2 * slots, 2 * hd), f32),
+            pltpu.VMEM((2 * slots, 2 * hd), f32),
+            pltpu.VMEM((n_rep, 2 * cap, hd), bf16),
+            pltpu.VMEM((n_tp,) + block, f32),
+            pltpu.VMEM((n_tp,) + block, bf16),
+            pltpu.VMEM((n_tp,) + block, bf16),
+            pltpu.VMEM((n_rep * n_tp,) + block, bf16),
+            pltpu.VMEM((reqs, width), bf16),
+            pltpu.VMEM((8, reqs), f32),
+            pltpu.VMEM((n_rep, 8, reqs), f32),
+            pltpu.VMEM((8, reqs), f32),
+            pltpu.VMEM((n_tp, 8, reqs), f32),
+            dma((7,)),
+            dma((2,)),
+            dma((2, n_rep)),
+            dma((2, n_rep)),
+            dma((n_rep,)),
+            dma((n_rep,)),
+            dma((2,)),
+            dma((2,)),
+            dma((n_tp,)),
+            dma((n_tp,)),
+            dma((4 * n_rep,)),
+            dma((4 * n_rep,)),
+            dma((n_rep + n_tp,)),
+            dma((n_rep + n_tp,)),
+        ],
+        compiler_params=pltpu.CompilerParams(
+            collective_id=0, has_side_effects=True, vmem_limit_bytes=40 * 1024 * 1024
+        ),
+    )(
+        pick,
+        hidden_in,
+        cosf,
+        sinf,
+        jnp.tile(home_lens, 4)[:, None],
+        onehot,
+        b_query[None],
+        b_key[None],
+        b_value[None],
+        gain_in[None],
+        gain_out[None],
+        k_cache[:, 0],
+        v_cache[:, 0],
+        w_query,
+        w_key,
+        w_value,
+        w_out,
+        w_head,
+    )
+    new = got_new.reshape(n_rep, 2, cap, hd)
+    new_k = new[:, 0].reshape(serve, hd)
+    new_v = new[:, 1].reshape(serve, hd)
+    targets = rep_pos * serve + jnp.arange(serve, dtype=jnp.int32)
+    equal = dest_flat[None, :] == targets[:, None]
+    lens = jnp.sum(jnp.where(equal, lengths[None, :] + 1, 0), axis=1) - 1
+    valid = lens >= 0
+    keys_served = write_newest(got_k, new_k, lens, valid, part)
+    values_served = write_newest(got_v, new_v, lens, valid, part)
+    share = serve // n_tp
+    wanted = (rep_pos * n_tp + tp_pos) * share + jnp.arange(share, dtype=jnp.int32)
+    final_norm = choose_own(best[1], wanted, dest_flat, f32)
+    top_logit = choose_own(best[0], wanted, dest_flat, f32)
+    return (final_norm, top_logit, keys_served[:, None], values_served[:, None])
+
+
 def solution(mesh):
     in_specs = (
         P("rep", None),
@@ -266,6 +779,7 @@
         P("rep", "tp", None, None),
         P("rep", "tp", None, None),
     )
+    small = mesh.shape["rep"] == 8 and mesh.shape["tp"] == 4
     return jax.shard_map(
-        per_device, mesh=mesh, in_specs=in_specs, out_specs=out_specs, check_vma=False
-    )
+        fast_device if small else per_device, mesh=mesh, in_specs=in_specs, out_specs=out_specs, check_vma=False
+    )

time: 176 us -> 98.5 us (0.56)
  Pallas kernels: 0 us -> 79.2 us
  waiting for transfers between devices: 68.5 us -> 0 us
  blocking collectives: 38.2 us -> 0 us
  starting transfers between devices: 18.6 us -> 0 us
  between operations: 14.3 us -> 0.89 us
  matrix products: 11.6 us -> 0 us
  other arithmetic: 18.1 us -> 6.73 us
  local copies, waits for them, and re-layouts: 6.22 us -> 11.1 us
    pallas_call x0 -> x1, Pallas kernels: none -> 79.2 us  [fast_device(): pl.pallas_call(functools.partial(fused, n_rep, n_tp), out_shape=[jax.Shap...]
    all_to_all x3 -> x0, waiting for transfers between devices: 55.1 us -> none  [spread(): return lax.all_to_all(item, axis, split_axis=0, concat_axis=0, tiled=True)]
    pmax x1 -> x0, blocking collectives: 38.2 us -> none  [per_device(): lax.pmax(jnp.stack([jnp.max(logits, axis=0), norm_all]), ('rep', 'tp'))]
    all_to_all x3 -> x0, starting transfers between devices: 16.7 us -> none  [spread(): return lax.all_to_all(item, axis, split_axis=0, concat_axis=0, tiled=True)]
    dot_general x8 -> x0, matrix products: 11.6 us -> none  [the longest x1 4.09 us: per_device(): lax.dot_general(w_head, lax.all_gather(normed, ('rep', 'tp'), axis=0, til...]
    reduce_scatter x1 -> x0, waiting for transfers between devices: 9.11 us -> none  [layer(): lax.psum_scatter(jnp.dot(attn, w_out, preferred_element_type=jnp.float32)...]
    unnamed x15 -> x19, local copies, waits for them, and re-layouts: 0.55 us -> 8.63 us
    gather x4 -> x0, local copies, waits for them, and re-layouts: 4.93 us -> none  [the longest x3 4.14 us: fill_buckets(): item[pick]]
  transfers between devices with their start and end apart: 11 -> 0, of which waited for: 6 -> 0; matrix products, arithmetic and copies ran while one was open for 14% -> 0% of each run, Pallas kernels for 0% -> 0%
where the time goes in v2:
time: 98.5 us; the launch traced here: 98 us
  Pallas kernels  79.2 us (80%)
  local copies, waits for them, and re-layouts  11.1 us (11%)
  other arithmetic  6.73 us (7%)
    pallas_call x1, Pallas kernels, fast_device(): pl.pallas_call(functools.partial(fused, n_rep, n_tp), out_shape=[jax.Shap...  79.2 us
    unnamed x19, local copies, waits for them, and re-layouts  8.63 us
    unnamed x1, other arithmetic  2.21 us

profile of v2, /device:TPU:0, one launch (start us, length us, event | category | flops | bytes accessed | tf_op | source)
XLA Modules:
  0.0 98.0 jit_solution(2146614487965439064)
XLA Ops:
  0.6 0.0 copy-start.7
  0.6 0.0 copy-start.6
  0.7 0.0 copy-start.4
  0.7 0.0 copy-start.3
  0.7 0.0 copy-start.5
  0.8 0.8 fusion.4
  1.6 0.7 broadcast_in_dim.116.bq
  2.3 0.5 broadcast.115
  2.8 1.3 %broadcast_multiply_fusion = (s32[256,1]{0,1:T(1,128)S(1)}, s32[256]{0:T(256)S(1)}) fusion(s32[256,1]{0,1:T(1,128)} %param.19, s32[]{:T(128)} %broadcast.115), kind=kLoop, calls=%fused_computation.30 | loop fusion | flops 256 | bytes 3076 | tf_op jit(solution)/shard_map/mul | solution.py:654
  4.1 0.1 add.96
  4.2 0.1 add.97
  4.3 0.1 eq.40
  4.4 0.3 convert_reduce_fusion
  4.7 0.1 reduce_sum.48
  4.8 0.7 add_add_fusion
  5.5 0.2 select_reduce_fusion
  5.6 0.1 select_reduce_fusion.1
  5.8 0.1 compare_and_fusion
  5.9 0.7 broadcast_in_dim.119.gin
  6.6 0.7 broadcast_in_dim.120.gout
  7.3 0.1 fusion.3
  7.5 0.1 pad_maximum_fusion
  7.5 0.1 broadcast_in_dim_tile.4.lens
  7.7 1.4 %copy.25.wk_hbm = bf16[3584,64]{1,0:T(8,128)(2,1)S(1)} copy(bf16[3584,64]{0,1:T(8,128)(2,1)} %param.22) | data formatting | bytes 917504 | tf_op args[7]
  9.1 1.4 %copy.26.wv_hbm = bf16[3584,64]{1,0:T(8,128)(2,1)S(1)} copy(bf16[3584,64]{0,1:T(8,128)(2,1)} %param.24) | data formatting | bytes 917504 | tf_op args[9]
  10.6 0.0 copy-start
  10.6 2.2 %copy-done = bf16[594,3584]{1,0:T(8,128)(2,1)S(1)} copy-done((bf16[594,3584]{1,0:T(8,128)(2,1)S(1)}, bf16[594,3584]{1,0:T(8,128)(2,1)}, u32[]{:S(2)}) %copy-start) | copy-done | bytes 4257816
  12.8 1.5 %copy-done.1 = bf16[3584,256]{1,0:T(8,128)(2,1)S(1)} copy-done((bf16[3584,256]{1,0:T(8,128)(2,1)S(1)}, bf16[3584,256]{1,0:T(8,128)(2,1)}, u32[]{:S(2)}) %copy-start.1) | copy-done | bytes 1835032
  14.3 1.5 %copy-done.2 = bf16[256,3584]{1,0:T(8,128)(2,1)S(1)} copy-done((bf16[256,3584]{1,0:T(8,128)(2,1)S(1)}, bf16[256,3584]{1,0:T(8,128)(2,1)}, u32[]{:S(2)}) %copy-start.2) | copy-done | bytes 1835032
  15.8 79.2 %shard_map.174 = (bf16[64,64,128]{2,1,0:T(8,128)(2,1)S(1)}, bf16[64,64,128]{2,1,0:T(8,128)(2,1)S(1)}, bf16[8,16,128]{2,1,0:T(8,128)(2,1)S(1)}, f32[8,256]{1,0:T(8,128)S(1)}) custom-call(s32[64]{0:T(128)S(1)} %broadcast_add_fusion.2.pick, bf16[32,3584]{1,0:T(8,128)(2,1)S(1)} %copy-done.5, f32[32,128]{1,0:T(8,128)S(1)} %get-tuple-element.35.cosf, ...), custom_call_target="tpu_custom_call" | custom-call | tf_op jit(solution)/shard_map/pallas_call | solution.py:670
  95.1 0.7 fusion.2
  95.8 2.2 %select_bitcast_fusion = (bf16[64,1,64,128]{3,2,1,0:T(8,128)(2,1)}, bf16[64,1,64,128]{3,2,1,0:T(8,128)(2,1)}) fusion(bf16[64,64,128]{2,1,0:T(8,128)(2,1)S(1)} %get-tuple-element.11, pred[64,64]{1,0:T(8,128)(4,1)S(1)} %compare_and_fusion, bf16[64,128]{1,0:T(8,128)(2,1)S(1)} %get-tuple-element.24, bf16[64,64,128]{2,1,0:T(8,128)(2,1)S(1)} %get-tuple-element.10, ...), kind=kLoop, calls=%fused_computation | loop fusion | flops 1048576 | bytes 4231168
  (23 shorter events, 0.1 us)
Async XLA Ops:
  0.6 9.9 %copy-start.7 = (bf16[64]{0:T(256)(128)(2,1)S(1)}, bf16[64]{0:T(256)(128)(2,1)}, u32[]{:S(2)}) copy-start(bf16[64]{0:T(256)(128)(2,1)} %param.25) | copy-start | bytes 388
  0.6 9.9 %copy-start.6 = (bf16[64]{0:T(256)(128)(2,1)S(1)}, bf16[64]{0:T(256)(128)(2,1)}, u32[]{:S(2)}) copy-start(bf16[64]{0:T(256)(128)(2,1)} %param.23) | copy-start | bytes 388
  0.7 9.9 %copy-start.4 = (bf16[32,1,64,128]{3,2,1,0:T(8,128)(2,1)S(1)}, bf16[32,1,64,128]{3,2,1,0:T(8,128)(2,1)}, u32[]{:S(2)}) copy-start(bf16[32,1,64,128]{3,2,1,0:T(8,128)(2,1)} %param.17) | copy-start | bytes 1572868
  0.7 9.9 %copy-start.3 = (bf16[32,1,64,128]{3,2,1,0:T(8,128)(2,1)S(1)}, bf16[32,1,64,128]{3,2,1,0:T(8,128)(2,1)}, u32[]{:S(2)}) copy-start(bf16[32,1,64,128]{3,2,1,0:T(8,128)(2,1)} %param.16) | copy-start | bytes 1572868
  0.7 9.9 %copy-start.5 = (bf16[32,3584]{1,0:T(8,128)(2,1)S(1)}, bf16[32,3584]{1,0:T(8,128)(2,1)}, u32[]{:S(2)}) copy-start(bf16[32,3584]{1,0:T(8,128)(2,1)} %hid.1) | copy-start | bytes 688132
  10.6 2.2 %copy-start = (bf16[594,3584]{1,0:T(8,128)(2,1)S(1)}, bf16[594,3584]{1,0:T(8,128)(2,1)}, u32[]{:S(2)}) copy-start(bf16[594,3584]{1,0:T(8,128)(2,1)} %wh_hbm.1) | copy-start | bytes 12773380
  12.8 1.5 %copy-start.1 = (bf16[3584,256]{1,0:T(8,128)(2,1)S(1)}, bf16[3584,256]{1,0:T(8,128)(2,1)}, u32[]{:S(2)}) copy-start(bf16[3584,256]{1,0:T(8,128)(2,1)} %wq_hbm.1) | copy-start | bytes 5505028
  14.3 1.5 %copy-start.2 = (bf16[256,3584]{1,0:T(8,128)(2,1)S(1)}, bf16[256,3584]{1,0:T(8,128)(2,1)}, u32[]{:S(2)}) copy-start(bf16[256,3584]{1,0:T(8,128)(2,1)} %wo_hbm.1) | copy-start | bytes 5505028

commit v3 on v2

--- a/solution.py
+++ b/solution.py
@@ -258,11 +258,7 @@
     sinf,
     lens,
     onehot,
-    bq,
-    bk,
-    bv,
-    gin,
-    gout,
+    vecs,
     k_hbm,
     v_hbm,
     wq_hbm,
@@ -366,20 +362,21 @@
         )
     pl.semaphore_wait(barrier, n_rep - 1 + n_tp - 1)
 
-    loads[0].wait()
-    loads[1].wait()
     sends = []
     own = pl.ds(rep * cap, cap)
-    for s in list(range(1, n_rep)) + [0]:
-        to = (rep + s) % n_rep
-        there = pl.ds(to * cap, cap)
-        for which, (src, buf, out) in enumerate(((kz, kb, out_k), (vz, vb, out_v))):
-
-            def fill(j, carry, src=src, buf=buf, to=to):
+    caches = ((kz, kb, out_k), (vz, vb, out_v))
+
+    def dispatch(which, shifts):
+        src, buf, out = caches[which]
+        for s in shifts:
+            to = (rep + s) % n_rep
+
+            def fill(j, carry, to=to):
                 buf[to * cap + j] = src[pick[to * cap + j]]
                 return carry
 
             lax.fori_loop(0, cap, fill, 0)
+            there = pl.ds(to * cap, cap)
             if s:
                 copy = remote(
                     buf.at[there], out.at[own], cs.at[which, s], cr.at[which, s], to, tp
@@ -387,28 +384,33 @@
             else:
                 copy = pltpu.make_async_copy(buf.at[own], out.at[own], keep_sem.at[which])
             copy.start()
-            sends.append((s, which, copy))
+            sends.append(copy)
+
+    loads[0].wait()
+    dispatch(0, (4, 3, 5, 2, 6, 1, 7, 0))
 
     xf = hid[...].astype(f32)
     xf_s[...] = xf
     scale_in = lax.rsqrt(jnp.mean(xf * xf, axis=1, keepdims=True) + eps)
-    normed_in = (xf * scale_in * gin[...].astype(f32)).astype(bf16)
+    normed_in = (xf * scale_in * vecs[:, :d]).astype(bf16)
     cos, sin = cosf[...], sinf[...]
 
     def turn(vals):
         return vals * cos + pltpu.roll(vals, hd // 2, 1) * sin
 
     loads[2].wait()
-    query = jnp.dot(normed_in, wq[...], preferred_element_type=f32) + bq[...].astype(f32)
+    query = jnp.dot(normed_in, wq[...], preferred_element_type=f32) + vecs[:, 2 * d : 2 * d + 2 * hd]
     loads[3].wait()
-    key_part = jnp.dot(normed_in, wk[...], preferred_element_type=f32) + bk[...].astype(f32)
+    across = (((1,), (1,)), ((), ()))
+    key_part = lax.dot_general(normed_in, wk[...], across, preferred_element_type=f32)
     loads[4].wait()
-    value_part = jnp.dot(normed_in, wv[...], preferred_element_type=f32) + bv[...].astype(f32)
+    value_part = lax.dot_general(normed_in, wv[...], across, preferred_element_type=f32)
+    new_part = jnp.concatenate([key_part, value_part], axis=1) + vecs[:, 2 * d + 2 * hd :]
     pair[c] = jnp.concatenate(
         [
             turn(query[:, :hd]),
             turn(query[:, hd:]),
-            jnp.concatenate([key_part, value_part], axis=1),
+            new_part,
         ],
         axis=0,
     ).astype(bf16)
@@ -443,6 +445,7 @@
     count = 4 * slots
     scale = 1.0 / hd**0.5
     keys = kz[0:slots].reshape(slots * half_len, hd)
+    loads[1].wait()
     values = vz[0:slots].reshape(slots * half_len, hd)
     scores = (
         lax.dot_general(
@@ -511,7 +514,7 @@
         (own_x + jnp.concatenate([summed[:rows], summed[rows:]], axis=1)).astype(bf16).astype(f32)
     )
     ms = jnp.mean(state * state, axis=1, keepdims=True)
-    normed = state * lax.rsqrt(ms + eps) * gout[...].astype(f32)
+    normed = state * lax.rsqrt(ms + eps) * vecs[:, d : 2 * d]
     ag[me] = jnp.concatenate([normed[:, :half_d], normed[:, half_d:]], axis=0).astype(bf16)
 
     x1, y1 = 1 - x, 1 - y
@@ -534,6 +537,7 @@
 
     for s in range(1, n_z):
         push(me, s, ((z + s) % n_z) * 2 + x, tp)
+    dispatch(1, range(2, n_rep, 2))
     plane = [(z + n_z - s) % n_z for s in range(n_z)]
     for s in range(n_z):
         block = (plane[s] * 2 + x) * n_tp + tp
@@ -547,6 +551,7 @@
         arrived(block, base_b + s)
         push(block, base_c + n_z + s, rep_second, tp_second)
         push(block, base_d + n_z + s, rep, mate)
+    dispatch(1, [3, 5, 1, 7, 0])
     for s in range(n_z):
         block = (plane[s] * 2 + x_second) * n_tp + tp_second
         arrived(block, base_c + s)
@@ -614,7 +619,7 @@
 
     for copy in new_sends:
         copy.wait()
-    for _, _, copy in sends:
+    for copy in sends:
         copy.wait()
 
 
@@ -675,7 +680,7 @@
             jax.ShapeDtypeStruct((n_rep, 2 * cap, hd), bf16),
             jax.ShapeDtypeStruct((8, reqs), f32),
         ],
-        in_specs=[pl.BlockSpec(memory_space=pltpu.SMEM)] + [vmem] * 10 + [anywhere] * 7,
+        in_specs=[pl.BlockSpec(memory_space=pltpu.SMEM)] + [vmem] * 6 + [anywhere] * 7,
         out_specs=[anywhere, anywhere, vmem, vmem],
         scratch_shapes=[
             pltpu.VMEM((slots + 1, half_len, hd), bf16),
@@ -683,8 +688,8 @@
             pltpu.VMEM((serve, half_len, hd), bf16),
             pltpu.VMEM((serve, half_len, hd), bf16),
             pltpu.VMEM(w_query.shape, bf16),
-            pltpu.VMEM(w_key.shape, bf16),
-            pltpu.VMEM(w_value.shape, bf16),
+            pltpu.VMEM(w_key.shape[::-1], bf16),
+            pltpu.VMEM(w_value.shape[::-1], bf16),
             pltpu.VMEM(w_out.shape, bf16),
             pltpu.VMEM(w_head.shape, bf16),
             pltpu.VMEM((slots, width), f32),
@@ -717,7 +722,7 @@
             dma((n_rep + n_tp,)),
         ],
         compiler_params=pltpu.CompilerParams(
-            collective_id=0, has_side_effects=True, vmem_limit_bytes=40 * 1024 * 1024
+            collective_id=0, has_side_effects=True, vmem_limit_bytes=60 * 1024 * 1024
         ),
     )(
         pick,
@@ -726,16 +731,12 @@
         sinf,
         jnp.tile(home_lens, 4)[:, None],
         onehot,
-        b_query[None],
-        b_key[None],
-        b_value[None],
-        gain_in[None],
-        gain_out[None],
+        jnp.concatenate([gain_in, gain_out, b_query, b_key, b_value]).astype(f32)[None],
         k_cache[:, 0],
         v_cache[:, 0],
         w_query,
-        w_key,
-        w_value,
+        w_key.T,
+        w_value.T,
         w_out,
         w_head,
     )

time: 98.5 us -> 84.7 us (0.86)
  Pallas kernels: 79.2 us -> 67.9 us
  local copies, waits for them, and re-layouts: 11.1 us -> 5.94 us
  other arithmetic: 6.73 us -> 9.68 us
    pallas_call x1, Pallas kernels: 79.2 us -> 67.9 us  [fast_device(): pl.pallas_call(functools.partial(fused, n_rep, n_tp), out_shape=[jax.Shap...]
    unnamed x19 -> x1, local copies, waits for them, and re-layouts: 8.63 us -> 0.51 us
    concatenate x0 -> x4, local copies, waits for them, and re-layouts: none -> 2.87 us  [fast_device(): jnp.concatenate([gain_in, gain_out, b_query, b_key, b_value]).astype(f32)]
    broadcast_in_dim x3 -> x0, local copies, waits for them, and re-layouts: 2.08 us -> none  [the longest x1 0.71 us: fast_device(): gain_in[None]]
where the time goes in v3:
time: 84.7 us; the launch traced here: 84.3 us
  Pallas kernels  67.9 us (80%)
  other arithmetic  9.68 us (11%)
  local copies, waits for them, and re-layouts  5.94 us (7%)
    pallas_call x1, Pallas kernels, fast_device(): pl.pallas_call(functools.partial(fused, n_rep, n_tp), out_shape=[jax.Shap...  67.9 us
    unnamed x1, other arithmetic  2.87 us
    concatenate x4, local copies, waits for them, and re-layouts, fast_device(): jnp.concatenate([gain_in, gain_out, b_query, b_key, b_value]).astype(f32)  2.87 us

profile of v3, /device:TPU:0, one launch (start us, length us, event | category | flops | bytes accessed | tf_op | source)
XLA Modules:
  0.0 84.3 jit_solution(13751445414061349624)
XLA Ops:
  0.7 0.8 fusion.4
  1.5 0.7 concatenate.30
  2.1 0.5 broadcast.115
  2.7 1.3 %broadcast_multiply_fusion = (s32[256,1]{0,1:T(1,128)S(1)}, s32[256]{0:T(256)S(1)}) fusion(s32[256,1]{0,1:T(1,128)} %param.19, s32[]{:T(128)} %broadcast.115), kind=kLoop, calls=%fused_computation.30 | loop fusion | flops 256 | bytes 3076 | tf_op jit(solution)/shard_map/mul | solution.py:659
  4.0 0.1 add.96
  4.1 0.1 add.97
  4.1 0.1 eq.40
  4.2 0.3 convert_reduce_fusion
  4.6 0.1 reduce_sum.48
  4.6 0.7 add_add_fusion
  5.3 0.2 select_reduce_fusion
  5.5 0.1 select_reduce_fusion.1
  5.6 0.5 broadcast_add_fusion.2.pick
  6.2 0.1 compare_and_fusion
  6.2 0.7 concatenate.28
  7.0 0.7 concatenate.29
  7.7 0.8 concatenate.33
  8.5 0.6 convert_element_type.22.vecs
  9.1 0.6 fusion.onehot
  9.7 0.1 fusion.3
  9.8 0.7 pad_maximum_fusion
  10.5 0.7 broadcast_in_dim_tile.4.lens
  11.3 67.9 %shard_map.174 = (bf16[64,64,128]{2,1,0:T(8,128)(2,1)}, bf16[64,64,128]{2,1,0:T(8,128)(2,1)}, bf16[8,16,128]{2,1,0:T(8,128)(2,1)}, f32[8,256]{1,0:T(8,128)}) custom-call(s32[64]{0:T(128)} %broadcast_add_fusion.2.pick, bf16[32,3584]{1,0:T(8,128)(2,1)} %hid.1, f32[32,128]{1,0:T(8,128)} %get-tuple-element.35.cosf, f32[32,128]{1,0:T(8,128)} %get-tuple-element.36.sinf, ...), custom_call_target="tpu_custom_call" | custom-call | tf_op jit(solution)/shard_map/pallas_call | solution.py:675
  79.2 0.8 fusion.5
  80.0 0.7 fusion.2
  80.7 0.7 slice_bitcast_fusion
  81.4 2.9 %select_bitcast_fusion = (bf16[64,1,64,128]{3,2,1,0:T(8,128)(2,1)}, bf16[64,1,64,128]{3,2,1,0:T(8,128)(2,1)}) fusion(bf16[64,64,128]{2,1,0:T(8,128)(2,1)} %get-tuple-element.11, pred[64,64]{1,0:T(8,128)(4,1)S(1)} %compare_and_fusion, bf16[64,128]{1,0:T(8,128)(2,1)S(1)} %get-tuple-element.24, bf16[64,64,128]{2,1,0:T(8,128)(2,1)} %get-tuple-element.10, ...), kind=kLoop, calls=%fused_computation | loop fusion | flops 1048576 | bytes 4231168
  (12 shorter events, 0.1 us)

commit v4 on v3

--- a/solution.py
+++ b/solution.py
@@ -1,4 +1,5 @@
 import functools
+import math
 
 import jax
 import jax.numpy as jnp
@@ -253,12 +254,13 @@
     n_rep,
     n_tp,
     pick,
+    lengths,
     hid,
-    cosf,
-    sinf,
-    lens,
-    onehot,
-    vecs,
+    gin,
+    gout,
+    bq,
+    bk,
+    bv,
     k_hbm,
     v_hbm,
     wq_hbm,
@@ -281,6 +283,7 @@
     wh,
     xf_s,
     pair,
+    new_s,
     mixed_s,
     mixed_r,
     nb,
@@ -322,6 +325,9 @@
     mate = tp + 1 - 2 * c
     me = rep * n_tp + tp
 
+    def vec(ref):
+        return ref[...].astype(f32)[None, :]
+
     def remote(src, dst, send, recv, rep_to, tp_to):
         return pltpu.make_async_remote_copy(
             src_ref=src,
@@ -392,20 +398,28 @@
     xf = hid[...].astype(f32)
     xf_s[...] = xf
     scale_in = lax.rsqrt(jnp.mean(xf * xf, axis=1, keepdims=True) + eps)
-    normed_in = (xf * scale_in * vecs[:, :d]).astype(bf16)
-    cos, sin = cosf[...], sinf[...]
+    normed_in = (xf * scale_in * vec(gin)).astype(bf16)
+    place = lax.broadcasted_iota(jnp.int32, (slots, hd), 0)
+    lens = jnp.zeros((slots, hd), jnp.int32)
+    for s in range(slots):
+        lens = jnp.where(place == s, lengths[rep * slots + s], lens)
+    entry = lax.broadcasted_iota(jnp.int32, (slots, hd), 1)
+    power = (entry % (hd // 2)).astype(f32) * (-2.0 / hd * math.log(1000000.0))
+    angle = lens.astype(f32) * jnp.exp(power)
+    cos, sin = jnp.cos(angle), jnp.sin(angle)
+    sin = jnp.where(entry < hd // 2, -sin, sin)
 
     def turn(vals):
         return vals * cos + pltpu.roll(vals, hd // 2, 1) * sin
 
     loads[2].wait()
-    query = jnp.dot(normed_in, wq[...], preferred_element_type=f32) + vecs[:, 2 * d : 2 * d + 2 * hd]
+    query = jnp.dot(normed_in, wq[...], preferred_element_type=f32) + vec(bq)
     loads[3].wait()
     across = (((1,), (1,)), ((), ()))
     key_part = lax.dot_general(normed_in, wk[...], across, preferred_element_type=f32)
     loads[4].wait()
     value_part = lax.dot_general(normed_in, wv[...], across, preferred_element_type=f32)
-    new_part = jnp.concatenate([key_part, value_part], axis=1) + vecs[:, 2 * d + 2 * hd :]
+    new_part = jnp.concatenate([key_part + vec(bk), value_part + vec(bv)], axis=1)
     pair[c] = jnp.concatenate(
         [
             turn(query[:, :hd]),
@@ -429,18 +443,23 @@
         [first[2 * slots :, hd // 2 :], second[2 * slots :, hd // 2 :]], axis=1
     )
     key_new = turn(key_raw).astype(bf16).astype(f32)
-    new_k = jnp.dot(onehot[...], key_new.astype(bf16), preferred_element_type=f32)
-    new_v = jnp.dot(onehot[...], value_new.astype(bf16), preferred_element_type=f32)
-    for t in range(n_rep):
-        cut = slice(t * cap, (t + 1) * cap)
-        nb[t] = jnp.concatenate([new_k[cut], new_v[cut]], axis=0).astype(bf16)
+    new_s[0:slots] = jnp.concatenate([key_new, value_new], axis=1)
+    new_s[slots : slots + 8] = jnp.zeros((8, 2 * hd), f32)
+
+    def fill_new(j, carry):
+        nb[pl.ds(j, 1)] = new_s[pl.ds(pick[j], 1)]
+        return carry
+
+    lax.fori_loop(0, n_rep * cap, fill_new, 0, unroll=8)
     new_sends = []
     for s in range(1, n_rep):
         to = (rep + s) % n_rep
-        copy = remote(nb.at[to], out_new.at[rep], ns.at[s], nr.at[s], to, tp)
+        copy = remote(
+            nb.at[pl.ds(to * cap, cap)], out_new.at[own], ns.at[s], nr.at[s], to, tp
+        )
         copy.start()
         new_sends.append(copy)
-    out_new[rep] = nb[rep]
+    out_new[own] = nb[own]
 
     count = 4 * slots
     scale = 1.0 / hd**0.5
@@ -455,7 +474,7 @@
     )
     row = lax.broadcasted_iota(jnp.int32, scores.shape, 0)
     col = lax.broadcasted_iota(jnp.int32, scores.shape, 1)
-    live = (col // half_len == row % slots) & (col % half_len + c * half_len < lens[...])
+    live = (col // half_len == row % slots) & (col % half_len + c * half_len < jnp.concatenate([lens[:, :1]] * 4, axis=0))
     scores = jnp.where(live, scores, -1e30)
     own_score = (
         jnp.sum(queries * jnp.concatenate([key_new] * 4, axis=0), axis=1, keepdims=True) * scale
@@ -514,7 +533,7 @@
         (own_x + jnp.concatenate([summed[:rows], summed[rows:]], axis=1)).astype(bf16).astype(f32)
     )
     ms = jnp.mean(state * state, axis=1, keepdims=True)
-    normed = state * lax.rsqrt(ms + eps) * vecs[:, d : 2 * d]
+    normed = state * lax.rsqrt(ms + eps) * vec(gout)
     ag[me] = jnp.concatenate([normed[:, :half_d], normed[:, half_d:]], axis=0).astype(bf16)
 
     x1, y1 = 1 - x, 1 - y
@@ -537,7 +556,6 @@
 
     for s in range(1, n_z):
         push(me, s, ((z + s) % n_z) * 2 + x, tp)
-    dispatch(1, range(2, n_rep, 2))
     plane = [(z + n_z - s) % n_z for s in range(n_z)]
     for s in range(n_z):
         block = (plane[s] * 2 + x) * n_tp + tp
@@ -546,12 +564,12 @@
         push(block, base_b + s, rep_first, tp_first)
         push(block, base_c + s, rep_second, tp_second)
         push(block, base_d + s, rep, mate)
+    dispatch(1, (4, 2, 6))
     for s in range(n_z):
         block = (plane[s] * 2 + x_first) * n_tp + tp_first
         arrived(block, base_b + s)
         push(block, base_c + n_z + s, rep_second, tp_second)
         push(block, base_d + n_z + s, rep, mate)
-    dispatch(1, [3, 5, 1, 7, 0])
     for s in range(n_z):
         block = (plane[s] * 2 + x_second) * n_tp + tp_second
         arrived(block, base_c + s)
@@ -560,6 +578,7 @@
         block = (plane[s] * 2 + x1) * n_tp + tp_y
         arrived(block, base_c + n_z + s)
         push(block, base_d + 3 * n_z + s, rep, mate)
+    dispatch(1, (3, 5, 1, 7, 0))
     other_y = mate + 2 - 4 * y
     x_first_m, x_second_m = x_second, x_first
     tp_first_m = c * mate + (1 - c) * other_y
@@ -660,13 +679,6 @@
     own_bucket = lax.dynamic_slice_in_dim(flat * cap + rank, rep_pos, 1, 0)[0]
     hits = own_bucket[None, :] == jnp.arange(serve, dtype=jnp.int32)[:, None]
     pick = slots + jnp.sum(jnp.where(hits, order[None, :] - slots, 0), axis=1)
-    onehot = hits.astype(jnp.bfloat16)
-    home_lens = lax.dynamic_slice_in_dim(lengths, rep_pos * slots, slots, 0)
-    freq = 1000000.0 ** (-(jnp.arange(hd // 2, dtype=jnp.float32) * 2.0 / hd))
-    angle = home_lens.astype(jnp.float32)[:, None] * freq
-    cos, sin = jnp.cos(angle), jnp.sin(angle)
-    cosf = jnp.concatenate([cos, cos], axis=1)
-    sinf = jnp.concatenate([-sin, sin], axis=1)
     bf16, f32 = jnp.bfloat16, jnp.float32
     vmem = pl.BlockSpec(memory_space=pltpu.VMEM)
     anywhere = pl.BlockSpec(memory_space=pl.ANY)
@@ -677,10 +689,10 @@
         out_shape=[
             jax.ShapeDtypeStruct((serve, half_len, hd), bf16),
             jax.ShapeDtypeStruct((serve, half_len, hd), bf16),
-            jax.ShapeDtypeStruct((n_rep, 2 * cap, hd), bf16),
+            jax.ShapeDtypeStruct((serve, 2 * hd), f32),
             jax.ShapeDtypeStruct((8, reqs), f32),
         ],
-        in_specs=[pl.BlockSpec(memory_space=pltpu.SMEM)] + [vmem] * 6 + [anywhere] * 7,
+        in_specs=[pl.BlockSpec(memory_space=pltpu.SMEM)] * 2 + [vmem] * 6 + [anywhere] * 7,
         out_specs=[anywhere, anywhere, vmem, vmem],
         scratch_shapes=[
             pltpu.VMEM((slots + 1, half_len, hd), bf16),
@@ -694,9 +706,10 @@
             pltpu.VMEM(w_head.shape, bf16),
             pltpu.VMEM((slots, width), f32),
             pltpu.VMEM((2, 3 * slots, hd), bf16),
+            pltpu.VMEM((slots + 8, 2 * hd), f32),
             pltpu.VMEM((2, 2 * slots, 2 * hd), f32),
             pltpu.VMEM((2 * slots, 2 * hd), f32),
-            pltpu.VMEM((n_rep, 2 * cap, hd), bf16),
+            pltpu.VMEM((serve, 2 * hd), f32),
             pltpu.VMEM((n_tp,) + block, f32),
             pltpu.VMEM((n_tp,) + block, bf16),
             pltpu.VMEM((n_tp,) + block, bf16),
@@ -726,12 +739,13 @@
         ),
     )(
         pick,
+        lengths,
         hidden_in,
-        cosf,
-        sinf,
-        jnp.tile(home_lens, 4)[:, None],
-        onehot,
-        jnp.concatenate([gain_in, gain_out, b_query, b_key, b_value]).astype(f32)[None],
+        gain_in,
+        gain_out,
+        b_query,
+        b_key,
+        b_value,
         k_cache[:, 0],
         v_cache[:, 0],
         w_query,
@@ -740,9 +754,8 @@
         w_out,
         w_head,
     )
-    new = got_new.reshape(n_rep, 2, cap, hd)
-    new_k = new[:, 0].reshape(serve, hd)
-    new_v = new[:, 1].reshape(serve, hd)
+    got_new = got_new.astype(bf16)
+    new_k, new_v = got_new[:, :hd], got_new[:, hd:]
     targets = rep_pos * serve + jnp.arange(serve, dtype=jnp.int32)
     equal = dest_flat[None, :] == targets[:, None]
     lens = jnp.sum(jnp.where(equal, lengths[None, :] + 1, 0), axis=1) - 1

time: 84.7 us -> 76.4 us (0.902)
  local copies, waits for them, and re-layouts: 5.94 us -> 1.61 us
  other arithmetic: 9.68 us -> 7.66 us
  Pallas kernels: 67.9 us -> 66.1 us
    concatenate x4 -> x0, local copies, waits for them, and re-layouts: 2.87 us -> none  [fast_device(): jnp.concatenate([gain_in, gain_out, b_query, b_key, b_value]).astype(f32)]
    pallas_call x1, Pallas kernels: 67.9 us -> 66.1 us  [fast_device(): pl.pallas_call(functools.partial(fused, n_rep, n_tp), out_shape=[jax.Shap...]
    convert_element_type x3 -> x1, other arithmetic: 2 us -> 0.84 us  [fast_device(): got_new = got_new.astype(bf16)]
where the time goes in v4:
time: 76.4 us; the launch traced here: 76.1 us
  Pallas kernels  66.1 us (87%)
  other arithmetic  7.66 us (10%)
  local copies, waits for them, and re-layouts  1.61 us (2%)
    pallas_call x1, Pallas kernels, fast_device(): pl.pallas_call(functools.partial(fused, n_rep, n_tp), out_shape=[jax.Shap...  66.1 us
    unnamed x1, other arithmetic  2.88 us

profile of v4, /device:TPU:0, one launch (start us, length us, event | category | flops | bytes accessed | tf_op | source)
XLA Modules:
  0.0 76.1 jit_solution(11052026514782965551)
XLA Ops:
  0.7 0.5 broadcast.104
  1.2 1.3 %broadcast_multiply_fusion = (s32[256,1]{0,1:T(1,128)S(1)}, s32[256]{0:T(256)S(1)}) fusion(s32[256,1]{0,1:T(1,128)} %param.19, s32[]{:T(128)} %broadcast.104), kind=kLoop, calls=%fused_computation.21 | loop fusion | flops 256 | bytes 3076 | tf_op jit(solution)/shard_map/mul | solution.py:678
  2.6 0.1 add.93
  2.6 0.1 add.94
  2.7 0.1 eq.40
  2.8 0.3 convert_reduce_fusion
  3.1 0.1 reduce_sum.48
  3.2 0.7 add_add_fusion
  3.9 0.1 select_reduce_fusion.1
  4.0 0.2 select_reduce_fusion
  4.2 0.5 broadcast_add_fusion.2.pick
  4.7 0.1 compare_and_fusion
  4.8 66.1 %shard_map.174 = (bf16[64,64,128]{2,1,0:T(8,128)(2,1)}, bf16[64,64,128]{2,1,0:T(8,128)(2,1)}, f32[64,256]{1,0:T(8,128)}, f32[8,256]{1,0:T(8,128)}) custom-call(s32[64]{0:T(128)} %broadcast_add_fusion.2.pick, s32[256]{0:T(256)} %lengths.1, bf16[32,3584]{1,0:T(8,128)(2,1)} %hid.1, bf16[3584]{0:T(1024)(128)(2,1)} %gin.1, bf16[3584]{0:T(1024)(128)(2,1)} %gout.1, ...), custom_call_target="tpu_custom_call" | custom-call | tf_op jit(solution)/shard_map/pallas_call | solution.py:687
  70.9 0.8 %fusion.3 = (f32[1,256]{1,0:T(1,128)S(1)}, f32[1,256]{1,0:T(1,128)S(1)}) fusion(f32[8,256]{1,0:T(8,128)} %get-tuple-element.8), kind=kLoop, calls=%fused_computation.26 | loop fusion | bytes 4096 | tf_op jit(solution)/shard_map/slice | solution.py:767
  71.7 0.7 fusion.1
  72.4 0.8 %convert_element_type.7 = bf16[64,256]{1,0:T(8,128)(2,1)S(1)} convert(f32[64,256]{1,0:T(8,128)} %get-tuple-element.9) | non-fusion elementwise | flops 16384 | bytes 98304 | tf_op jit(solution)/shard_map/convert_element_type | solution.py:757
  73.2 2.9 %select_bitcast_fusion = (bf16[64,1,64,128]{3,2,1,0:T(8,128)(2,1)}, bf16[64,1,64,128]{3,2,1,0:T(8,128)(2,1)}) fusion(bf16[64,64,128]{2,1,0:T(8,128)(2,1)} %get-tuple-element.11, pred[64,64]{1,0:T(8,128)(4,1)S(1)} %compare_and_fusion, bf16[64,128]{1,0:T(8,128)(2,1)S(1)} %get-tuple-element.22, bf16[64,64,128]{2,1,0:T(8,128)(2,1)} %get-tuple-element.10, ...), kind=kLoop, calls=%fused_computation | loop fusion | flops 1048576 | bytes 4231168
  (11 shorter events, 0.1 us)

commit v5 on v4

--- a/solution.py
+++ b/solution.py
@@ -270,7 +270,8 @@
     wh_hbm,
     out_k,
     out_v,
-    out_new,
+    out_nk,
+    out_nv,
     out_max,
     kz,
     vz,
@@ -284,6 +285,7 @@
     xf_s,
     pair,
     new_s,
+    new_r,
     mixed_s,
     mixed_r,
     nb,
@@ -455,11 +457,11 @@
     for s in range(1, n_rep):
         to = (rep + s) % n_rep
         copy = remote(
-            nb.at[pl.ds(to * cap, cap)], out_new.at[own], ns.at[s], nr.at[s], to, tp
+            nb.at[pl.ds(to * cap, cap)], new_r.at[own], ns.at[s], nr.at[s], to, tp
         )
         copy.start()
         new_sends.append(copy)
-    out_new[own] = nb[own]
+    new_r[own] = nb[own]
 
     count = 4 * slots
     scale = 1.0 / hd**0.5
@@ -638,6 +640,8 @@
 
     for copy in new_sends:
         copy.wait()
+    out_nk[...] = new_r[:, :hd].astype(bf16)
+    out_nv[...] = new_r[:, hd:].astype(bf16)
     for copy in sends:
         copy.wait()
 
@@ -684,16 +688,17 @@
     anywhere = pl.BlockSpec(memory_space=pl.ANY)
     dma = pltpu.SemaphoreType.DMA
     block = (2 * rows, width // 2)
-    got_k, got_v, got_new, best = pl.pallas_call(
+    got_k, got_v, new_k, new_v, best = pl.pallas_call(
         functools.partial(fused, n_rep, n_tp),
         out_shape=[
             jax.ShapeDtypeStruct((serve, half_len, hd), bf16),
             jax.ShapeDtypeStruct((serve, half_len, hd), bf16),
-            jax.ShapeDtypeStruct((serve, 2 * hd), f32),
+            jax.ShapeDtypeStruct((serve, hd), bf16),
+            jax.ShapeDtypeStruct((serve, hd), bf16),
             jax.ShapeDtypeStruct((8, reqs), f32),
         ],
         in_specs=[pl.BlockSpec(memory_space=pltpu.SMEM)] * 2 + [vmem] * 6 + [anywhere] * 7,
-        out_specs=[anywhere, anywhere, vmem, vmem],
+        out_specs=[anywhere, anywhere, vmem, vmem, vmem],
         scratch_shapes=[
             pltpu.VMEM((slots + 1, half_len, hd), bf16),
             pltpu.VMEM((slots + 1, half_len, hd), bf16),
@@ -707,6 +712,7 @@
             pltpu.VMEM((slots, width), f32),
             pltpu.VMEM((2, 3 * slots, hd), bf16),
             pltpu.VMEM((slots + 8, 2 * hd), f32),
+            pltpu.VMEM((serve, 2 * hd), f32),
             pltpu.VMEM((2, 2 * slots, 2 * hd), f32),
             pltpu.VMEM((2 * slots, 2 * hd), f32),
             pltpu.VMEM((serve, 2 * hd), f32),
@@ -754,8 +760,6 @@
         w_out,
         w_head,
     )
-    got_new = got_new.astype(bf16)
-    new_k, new_v = got_new[:, :hd], got_new[:, hd:]
     targets = rep_pos * serve + jnp.arange(serve, dtype=jnp.int32)
     equal = dest_flat[None, :] == targets[:, None]
     lens = jnp.sum(jnp.where(equal, lengths[None, :] + 1, 0), axis=1) - 1
@@ -764,8 +768,9 @@
     values_served = write_newest(got_v, new_v, lens, valid, part)
     share = serve // n_tp
     wanted = (rep_pos * n_tp + tp_pos) * share + jnp.arange(share, dtype=jnp.int32)
-    final_norm = choose_own(best[1], wanted, dest_flat, f32)
-    top_logit = choose_own(best[0], wanted, dest_flat, f32)
+    here = dest_flat[None, :] == wanted[:, None]
+    chosen = jnp.sum(jnp.where(here[None], best[:2, None, :], 0.0), axis=2)
+    top_logit, final_norm = chosen[0], chosen[1]
     return (final_norm, top_logit, keys_served[:, None], values_served[:, None])
 
 

time: 76.4 us -> 75.4 us (0.987)
  other arithmetic: 7.66 us -> 6.3 us
    convert_element_type x1 -> x0, other arithmetic: 0.84 us -> none  [fast_device(): got_new = got_new.astype(bf16)]
where the time goes in v5:
time: 75.4 us; the launch traced here: 75.2 us
  Pallas kernels  66.1 us (88%)
  other arithmetic  6.3 us (8%)
  local copies, waits for them, and re-layouts  2.05 us (3%)
    pallas_call x1, Pallas kernels, fast_device(): pl.pallas_call(functools.partial(fused, n_rep, n_tp), out_shape=[jax.Shap...  66.1 us
    unnamed x1, other arithmetic  2.9 us

profile of v5, /device:TPU:0, one launch (start us, length us, event | category | flops | bytes accessed | tf_op | source)
XLA Modules:
  0.0 75.2 jit_solution(8363428105334706573)
XLA Ops:
  0.7 0.5 broadcast.123
  1.2 1.3 %broadcast_multiply_fusion = (s32[256,1]{0,1:T(1,128)S(1)}, s32[256]{0:T(256)S(1)}) fusion(s32[256,1]{0,1:T(1,128)} %param.19, s32[]{:T(128)} %broadcast.123), kind=kLoop, calls=%fused_computation.21 | loop fusion | flops 256 | bytes 3076 | tf_op jit(solution)/shard_map/mul | solution.py:682
  2.6 0.1 add.93
  2.6 0.1 add.94
  2.7 0.1 eq.86
  2.8 0.3 convert_reduce_fusion
  3.1 0.1 reduce_sum.39
  3.2 0.7 add_add_fusion
  3.9 0.1 select_reduce_fusion.2
  4.0 0.2 select_reduce_fusion
  4.2 0.5 broadcast_add_fusion.2.pick
  4.7 0.1 broadcast_compare_fusion
  4.8 0.1 compare_and_fusion
  4.9 66.1 %shard_map.174 = (bf16[64,64,128]{2,1,0:T(8,128)(2,1)}, bf16[64,64,128]{2,1,0:T(8,128)(2,1)}, bf16[64,128]{1,0:T(8,128)(2,1)}, bf16[64,128]{1,0:T(8,128)(2,1)}, f32[8,256]{1,0:T(8,128)}) custom-call(s32[64]{0:T(128)} %broadcast_add_fusion.2.pick, s32[256]{0:T(256)} %lengths.1, bf16[32,3584]{1,0:T(8,128)(2,1)} %hid.1, bf16[3584]{0:T(1024)(128)(2,1)} %gin.1, ...), custom_call_target="tpu_custom_call" | custom-call | tf_op jit(solution)/shard_map/pallas_call | solution.py:691
  71.0 0.7 slice.9
  71.7 0.1 select_reduce_fusion.1
  71.8 0.5 slice_bitcast_fusion
  72.3 2.9 %select_bitcast_fusion = (bf16[64,1,64,128]{3,2,1,0:T(8,128)(2,1)}, bf16[64,1,64,128]{3,2,1,0:T(8,128)(2,1)}) fusion(bf16[64,64,128]{2,1,0:T(8,128)(2,1)} %get-tuple-element.13, pred[64,64]{1,0:T(8,128)(4,1)S(1)} %compare_and_fusion, bf16[64,128]{1,0:T(8,128)(2,1)} %get-tuple-element.12, bf16[64,64,128]{2,1,0:T(8,128)(2,1)} %get-tuple-element.11, ...), kind=kLoop, calls=%fused_computation | loop fusion | flops 1048576 | bytes 4231168
  (10 shorter events, 0.1 us)
